TPU v7x, 256 devices: a whole 4x4x8 slice. The times are simulated.
256 devices in a mesh: seq: 64 (over y, z, core), fsdp: 4 (over x).
Axes of the slice: x: 4, y: 4, z: 8, core: 2. Of those that a mesh axis runs over, the one named last changes fastest.
Arguments:
- tokens: bfloat16 [65536, 4096], P('seq', 'fsdp'), may hold values from -6 to 6
- projection: bfloat16 [3, 4096, 2048], P(None, 'seq', 'fsdp'), may hold values from -0.09375 to 0.09375
- log_decay: float32 [65536, 16], P('seq', 'fsdp'), may hold values from -2 to 0, as said below
Outputs:
- attended: bfloat16 [65536, 2048], P('seq', 'fsdp')
Inputs may be any that keep to these rules, and one draw needn't show every extreme that they name: `log_decay`: negative logarithms of decay factors, one for each position and head.
All inputs are finite; a program needn't handle non-finite values.
Results may differ from a plain program's by a relative error of at most 0.006.
Values may be sent and summed in bfloat16 or wider, within the bound.
No kernel may reach another device: no remote copies, remote signals or barrier semaphores. Data moves between devices by JAX's collectives and lax.ppermute only.
A program may use at most 64 MiB of HBM per device.

v0:
```python
import jax
import jax.numpy as jnp
from jax import lax
from jax.sharding import PartitionSpec as P

BLK = 512


def entering(part, axis, combine, identity):
    place = lax.axis_index(axis)
    gathered = jax.tree.map(lambda a: lax.all_gather(a, axis), part)
    state = jax.tree.map(lambda a, e: jnp.zeros_like(a) + jnp.asarray(e, a.dtype), part, identity)

    def one(hop, state):
        return combine(
            state, jax.tree.map(lambda a: lax.dynamic_index_in_dim(a, hop, 0, False), gathered)
        )

    return lax.fori_loop(0, place, one, state)


def local_states(key_vecs, value_vecs, decay):
    running = jnp.cumsum(decay, axis=1)
    last = running[:, -1]
    carried = key_vecs.astype(jnp.float32) * jnp.exp(last[:, None, :] - running)[..., None]
    fresh = jnp.einsum(
        "nshd,nshe->nhde", carried, value_vecs.astype(jnp.float32), precision=lax.Precision.HIGHEST
    )

    def advance(state, inputs):
        block_last, block_fresh = inputs
        return (jnp.exp(block_last)[:, None, None] * state + block_fresh, state)

    start = jnp.zeros(fresh.shape[1:], jnp.float32)
    final, before = lax.scan(advance, start, (last, fresh))
    leading = jnp.cumsum(last, axis=0) - last
    whole_decay = jnp.exp(jnp.sum(last, axis=0))
    return (final, before, leading, whole_decay)


def combine(earlier, later):
    return (earlier[0] * later[0], later[0][:, None, None] * earlier[1] + later[1])


def chain(key_raw, value_raw, decay, shaped):
    key_vecs = shaped(jax.nn.silu(key_raw).astype(jnp.bfloat16))
    value_vecs = shaped(value_raw.astype(jnp.bfloat16))
    final, before, leading, whole_decay = local_states(key_vecs, value_vecs, decay)
    identity = (jnp.ones_like(whole_decay), jnp.zeros_like(final))
    carry = entering((whole_decay, final), "seq", combine, identity)
    incoming = before + jnp.exp(leading)[:, :, None, None] * carry[1][None]
    return (key_vecs, value_vecs, incoming)


def attend_block(inputs):
    queries, key_vecs, value_vecs, decay, state = inputs
    running = jnp.cumsum(decay, axis=0)
    across = running.T
    gap = across[:, :, None] - across[:, None, :]
    lower = jnp.arange(gap.shape[1])[:, None] >= jnp.arange(gap.shape[2])[None, :]
    fading = jnp.exp(jnp.where(lower[None], gap, -1e30))
    scores = jnp.einsum("thd,shd->hts", queries, key_vecs, preferred_element_type=jnp.float32)
    weights = (fading * scores).astype(jnp.bfloat16)
    intra = jnp.einsum("hts,she->the", weights, value_vecs, preferred_element_type=jnp.float32)
    inter = jnp.exp(running)[:, :, None] * jnp.einsum(
        "thd,hde->the", queries.astype(jnp.float32), state, precision=lax.Precision.HIGHEST
    )
    mixed = intra + inter
    normed = mixed * lax.rsqrt(jnp.mean(mixed * mixed, axis=-1, keepdims=True) + 1e-06)
    return normed.astype(jnp.bfloat16)


def on_device(tokens, projection, log_decay):
    features = lax.all_gather(tokens, "fsdp", axis=1, tiled=True)
    rows = features.shape[0]
    heads = log_decay.shape[1]
    width = projection.shape[2]
    head = width // heads
    blocks = rows // BLK

    def shaped(matrix):
        return matrix.reshape(blocks, BLK, heads, head)

    decay = log_decay.reshape(blocks, BLK, heads)
    raw = jnp.einsum(
        "td,cdn->ctn",
        features,
        lax.all_gather(projection, "seq", axis=1, tiled=True),
        preferred_element_type=jnp.float32,
    )
    key_vecs, value_vecs, incoming = chain(raw[1], raw[2], decay, shaped)
    query_raw = raw[0]
    queries = shaped(jax.nn.silu(query_raw).astype(jnp.bfloat16))
    outputs = lax.map(attend_block, (queries, key_vecs, value_vecs, decay, incoming))
    return outputs.reshape(rows, width)


def solution(mesh):
    in_specs = (P("seq", "fsdp"), P(None, "seq", "fsdp"), P("seq", "fsdp"))
    out_specs = P("seq", "fsdp")
    return jax.shard_map(
        on_device, mesh=mesh, in_specs=in_specs, out_specs=out_specs, check_vma=False
    )
```

profile of v0, /device:TPU:249, one launch (start us, length us, event | category | flops | bytes accessed | tf_op | source)
XLA Modules:
  0.0 447.1 jit_solution(9601108571453135276)
XLA Ops:
  8.1 2.4 reduce-window.14
  11.5 83.5 %all-gather.8.cloned.1.call-done = bf16[1024,4096]{1,0:T(8,128)(2,1)} async-done(((bf16[1024,1024]{1,0:T(8,128)(2,1)}), bf16[1024,4096]{1,0:T(8,128)(2,1)}) %all-gather.8.cloned.1.call-update) | async-done | bytes 8388624 | tf_op jit(solution)/shard_map/all_gather | solution.py:74
  95.0 90.9 %all-gather.6.cloned.1.call-done = bf16[3,4096,512]{2,1,0:T(8,128)(2,1)} async-done(((bf16[3,64,512]{2,1,0:T(8,128)(2,1)}), bf16[3,4096,512]{2,1,0:T(8,128)(2,1)}) %all-gather.6.cloned.1.call-update) | async-done | bytes 12582928 | tf_op jit(solution)/shard_map/all_gather | solution.py:88
  185.9 17.3 %fusion.27 = f32[3,1024,512]{1,2,0:T(8,128)S(1)} fusion(bf16[3,4096,512]{2,1,0:T(8,128)(2,1)} %all-gather.6.cloned.1.call-done, bf16[1024,4096]{1,0:T(8,128)(2,1)} %all-gather.8.cloned.1.call-done), kind=kOutput, calls=%fused_computation.39 | convolution fusion | flops 12884901888 | bytes 27262976 | tf_op jit(solution)/shard_map/td,cdn->ctn/dot_general | solution.py:85
  203.3 1.8 fusion.35
  205.1 1.6 convert_element_type.24
  206.7 2.8 squeeze.42
  209.4 2.8 copy.51
  212.2 4.0 squeeze.41
  216.2 4.1 copy.49
  220.3 2.8 multiply_convert_fusion.2
  223.1 2.7 fusion.30
  228.3 124.5 %all-reduce = f32[256]{0:T(256)S(1)} all-reduce(f32[256]{0:T(256)S(1)} %exponential_dynamic-update-slice_fusion), channel_id=2, replica_groups=mesh['seq'=64,'fsdp'=4] {'seq'}, use_global_device_ids=true, to_apply=%add | all-reduce | flops 256 | bytes 2048
  353.0 1.2 copy.54
  354.2 69.7 %while.35 = (s32[]{:T(128)}, f32[4,128,128]{2,1,0:T(8,128)S(1)}, s32[]{:T(128)}, f32[64,4]{1,0:T(8,128)S(1)}, f32[64,4,128,128]{3,2,1,0:T(8,128)}, /*index=5*/s32[]{:T(128)}, s32[]{:T(128)}, s32[]{:T(128)}) while((s32[]{:T(128)}, f32[4,128,128]{2,1,0:T(8,128)S(1)}, s32[]{:T(128)}, f32[64,4]{1,0:T(8,128)S(1)}, f32[64,4,128,128]{3,2,1,0:T(8,128)}, ...), condition=%wide.region_7.8_spmd, body=%wide.region_6.7_spmd.sunk | while | flops 131077 | bytes 786615 | solution.py:19
  354.2 1.1 bitcast_add_fusion.4
  355.3 1.1 bitcast_add_fusion.4
  356.4 1.1 bitcast_add_fusion.4
  357.5 1.1 bitcast_add_fusion.4
  358.6 1.1 bitcast_add_fusion.4
  359.7 1.1 bitcast_add_fusion.4
  360.8 1.1 bitcast_add_fusion.4
  361.9 1.1 bitcast_add_fusion.4
  363.0 1.1 bitcast_add_fusion.4
  364.1 1.1 bitcast_add_fusion.4
  368.5 1.1 bitcast_add_fusion.4
  369.6 1.1 bitcast_add_fusion.4
  370.7 1.1 bitcast_add_fusion.4
  371.9 1.1 bitcast_add_fusion.4
  373.0 1.1 bitcast_add_fusion.4
  374.1 1.1 bitcast_add_fusion.4
  378.5 1.1 bitcast_add_fusion.4
  379.6 1.1 bitcast_add_fusion.4
  380.7 1.1 bitcast_add_fusion.4
  381.8 1.1 bitcast_add_fusion.4
  382.9 1.1 bitcast_add_fusion.4
  384.0 1.1 bitcast_add_fusion.4
  389.5 1.1 bitcast_add_fusion.4
  390.6 1.1 bitcast_add_fusion.4
  391.7 1.1 bitcast_add_fusion.4
  392.8 1.1 bitcast_add_fusion.4
  393.9 1.1 bitcast_add_fusion.4
  395.0 1.1 bitcast_add_fusion.4
  399.4 1.1 bitcast_add_fusion.4
  400.5 1.1 bitcast_add_fusion.4
  401.6 1.1 bitcast_add_fusion.4
  402.7 1.1 bitcast_add_fusion.4
  403.8 1.1 bitcast_add_fusion.4
  404.9 1.1 bitcast_add_fusion.4
  410.5 1.1 bitcast_add_fusion.4
  411.6 1.1 bitcast_add_fusion.4
  412.7 1.1 bitcast_add_fusion.4
  413.8 1.1 bitcast_add_fusion.4
  414.9 1.1 bitcast_add_fusion.4
  416.0 1.1 bitcast_add_fusion.4
  420.4 1.1 bitcast_add_fusion.4
  421.5 1.1 bitcast_add_fusion.4
  422.6 1.1 bitcast_add_fusion.4
  424.0 14.2 %while.36 = (s32[]{:T(128)}, bf16[2,512,4,128]{3,2,1,0:T(4,128)(2,1)}, bf16[2,512,4,128]{1,3,2,0:T(8,128)(2,1)}, f32[2,512,4]{1,2,0:T(4,128)S(1)}, bf16[2,512,4,...) while((s32[]{:T(128)}, ...), condition=%wide.region_12.13_spmd, body=%wide.region_8.12_spmd.sunk | while | flops 945817664 | bytes 9857989 | solution.py:94
  424.0 1.2 reduce-window.24
  425.8 3.1 fusion.46
  431.1 1.2 reduce-window.24
  432.9 3.1 fusion.46
  438.2 2.4 copy.70
  (156 shorter events, 32.3 us)
Async XLA Ops:
  6.5 1.5 copy-start.5
  6.5 88.4 %all-gather.8.cloned.1.call-start = ((), (), s32[]{:S(2)}) async-start(), calls=%async_computation.1 | async-start | bytes 10485760 | tf_op jit(solution)/shard_map/all_gather | solution.py:74
  7.3 178.6 %all-gather.6.cloned.1.call-start = ((), (), s32[]{:S(2)}) async-start(), calls=%async_computation | async-start | bytes 12779520 | tf_op jit(solution)/shard_map/all_gather | solution.py:88
  8.0 346.1 %all-gather.10.cloned.1.call-start = ((), (), s32[]{:S(2)}) async-start(), calls=%async_computation.2 | async-start | bytes 17039360 | tf_op jit(solution)/shard_map/all_gather | solution.py:11
  220.3 2.8 copy-start.1
  223.1 2.8 copy-start.3
  223.1 2.8 copy-start.4
  225.9 1.2 copy-start.6
  225.9 127.1 %copy-start.2 = (bf16[2,512,4,128]{1,0,3,2:T(2,128)(2,1)S(1)}, bf16[2,512,4,128]{1,0,3,2:T(2,128)(2,1)}, u32[]{:S(2)}) copy-start(bf16[2,512,4,128]{1,0,3,2:T(2,128)(2,1)} %convert_element_type.24) | copy-start | bytes 3145732
  226.3 0.7 copy-start
Sparse Core Ops, SparseCore 0:
  9.2 85.7 all-gather.7
  97.8 88.0 all-gather.5
  227.1 96.5 all-gather.9
where the time goes:
time: 449 us; the launch traced here: 447 us
  waiting for transfers between devices  176 us (39%)
  blocking collectives  125 us (28%)
  other arithmetic  76.6 us (17%)
  matrix products  27.7 us (6%)
  local copies, waits for them, and re-layouts  26.2 us (6%)
  between operations  13.9 us (3%)
    unnamed x1, blocking collectives  125 us
    all_gather x1, waiting for transfers between devices, on_device(): lax.all_gather(projection, 'seq', axis=1, tiled=True)  90.9 us
    all_gather x1, waiting for transfers between devices, on_device(): features = lax.all_gather(tokens, 'fsdp', axis=1, tiled=True)  83.5 us
    add x63, other arithmetic, combine(): later[0][:, None, None] * earlier[1] + later[1]  66.8 us
    dot_general x1, matrix products, on_device(): jnp.einsum('td,cdn->ctn', features, lax.all_gather(projection, 'seq', axi...  17.3 us
  transfers between devices with their start and end apart: 3, of which 2 were waited for; matrix products, arithmetic and copies ran while one was open for 1% of the time, Pallas kernels for 0%

commit v1 on v0

v1 whole, which is shorter than its diff:
```python
import functools

import jax
import jax.numpy as jnp
from jax import lax
from jax.experimental import pallas as pl
from jax.experimental.pallas import tpu as pltpu
from jax.sharding import PartitionSpec as P

BLK = 512
HEAD = 128
F32 = jnp.float32
BF16 = jnp.bfloat16
EXACT = lax.Precision.HIGHEST
VMEM_LIMIT = 56 * 2**20


def silu(v):
    return v / (1.0 + jnp.exp(-v))


def project(step, tokens, weights, acc):
    for d in range(4):

        @pl.when(step == d)
        def _(d=d):
            for c in range(weights.shape[0]):
                part = jnp.dot(tokens[d][...], weights[c], preferred_element_type=F32)
                acc[c] = part if d == 0 else acc[c] + part


def kv_kernel(order, own, left, right, far, weights, run, last, k_out, v_out, fresh, acc):
    step = pl.program_id(0)
    project(step, (own, left, right, far), weights, acc)

    @pl.when(step == 3)
    def _():
        for h in range(4):
            cols = slice(h * HEAD, (h + 1) * HEAD)
            k = silu(acc[0, :, cols]).astype(BF16)
            v = acc[1, :, cols].astype(BF16)
            k_out[:, cols] = k
            v_out[:, cols] = v
            fade = jnp.exp(last[:, h : h + 1] - run[:, h : h + 1])
            carried = (k.astype(F32) * fade).astype(BF16)
            fresh[h] = lax.dot_general(
                carried, v, (((0,), (0,)), ((), ())), preferred_element_type=F32
            )


def q_kernel(order, own, left, right, far, weights, run, across, k, v, q_out, intra, acc):
    step = pl.program_id(0)
    project(step, (own, left, right, far), weights, acc)

    @pl.when(step == 3)
    def _():
        half = BLK // 2
        for h in range(4):
            cols = slice(h * HEAD, (h + 1) * HEAD)
            q = silu(acc[0, :, cols]).astype(BF16)
            q_out[:, cols] = q
            for t in range(2):
                rows = slice(t * half, (t + 1) * half)
                wide = (t + 1) * half
                scores = lax.dot_general(
                    q[rows],
                    k[:wide, cols],
                    (((1,), (1,)), ((), ())),
                    preferred_element_type=F32,
                )
                gap = run[rows, h : h + 1] - across[h : h + 1, :wide]
                at = lax.broadcasted_iota(jnp.int32, gap.shape, 0) + t * half
                lower = at >= lax.broadcasted_iota(jnp.int32, gap.shape, 1)
                fading = jnp.exp(jnp.where(lower, gap, -1e30))
                mix = (fading * scores).astype(BF16)
                intra[rows, cols] = jnp.dot(mix, v[:wide, cols], preferred_element_type=F32)


def final_kernel(q, intra, run, state, out):
    for h in range(4):
        cols = slice(h * HEAD, (h + 1) * HEAD)
        whole = state[0, h]
        high = whole.astype(BF16)
        low = (whole - high.astype(F32)).astype(BF16)
        inter = jnp.dot(q[:, cols], high, preferred_element_type=F32)
        inter += jnp.dot(q[:, cols], low, preferred_element_type=F32)
        mixed = intra[:, cols] + jnp.exp(run[:, h : h + 1]) * inter
        scale = lax.rsqrt(jnp.mean(mixed * mixed, axis=-1, keepdims=True) + 1e-06)
        out[:, cols] = (mixed * scale).astype(BF16)


def params():
    return pltpu.CompilerParams(
        dimension_semantics=("arbitrary",), vmem_limit_bytes=VMEM_LIMIT
    )


def token_specs(block):
    spec = pl.BlockSpec((BLK, 1024), lambda d, order: (block, 0))
    return [spec, spec, spec, pl.BlockSpec((BLK, 1024), lambda d, order: (0, 0))]


def fixed(shape):
    return pl.BlockSpec(shape, lambda d, order: (0,) * len(shape))


def project_kv(block, order, tokens, weights, run, last):
    width = weights.shape[2]
    return pl.pallas_call(
        kv_kernel,
        grid_spec=pltpu.PrefetchScalarGridSpec(
            num_scalar_prefetch=1,
            grid=(4,),
            in_specs=[
                *token_specs(block),
                pl.BlockSpec((2, 1024, width), lambda d, order: (0, order[d], 0)),
                fixed((BLK, 4)),
                fixed((1, 4)),
            ],
            out_specs=[fixed((BLK, width)), fixed((BLK, width)), fixed((4, HEAD, HEAD))],
            scratch_shapes=[pltpu.VMEM((2, BLK, width), F32)],
        ),
        out_shape=[
            jax.ShapeDtypeStruct((BLK, width), BF16),
            jax.ShapeDtypeStruct((BLK, width), BF16),
            jax.ShapeDtypeStruct((4, HEAD, HEAD), F32),
        ],
        compiler_params=params(),
        cost_estimate=pl.CostEstimate(
            flops=2 * BLK * 4096 * 1024, bytes_accessed=14 * 2**20, transcendentals=BLK * 512
        ),
        name=f"kv{block}",
    )(order, *tokens, weights, run, last)


def project_q(block, order, tokens, weights, run, across, k, v):
    width = weights.shape[2]
    return pl.pallas_call(
        q_kernel,
        grid_spec=pltpu.PrefetchScalarGridSpec(
            num_scalar_prefetch=1,
            grid=(4,),
            in_specs=[
                *token_specs(block),
                pl.BlockSpec((1, 1024, width), lambda d, order: (0, order[d], 0)),
                fixed((BLK, 4)),
                fixed((4, BLK)),
                fixed((BLK, width)),
                fixed((BLK, width)),
            ],
            out_specs=[fixed((BLK, width)), fixed((BLK, width))],
            scratch_shapes=[pltpu.VMEM((1, BLK, width), F32)],
        ),
        out_shape=[
            jax.ShapeDtypeStruct((BLK, width), BF16),
            jax.ShapeDtypeStruct((BLK, width), F32),
        ],
        compiler_params=params(),
        cost_estimate=pl.CostEstimate(
            flops=2 * BLK * 4096 * 512, bytes_accessed=10 * 2**20, transcendentals=BLK * BLK * 4
        ),
        name=f"q{block}",
    )(order, *tokens, weights, run, across, k, v)


def finish(q, intra, run, states):
    width = q[0].shape[1]
    rows = 2 * BLK

    def body(q0, q1, i0, i1, run, state, out):
        for b, (qb, ib) in enumerate(((q0, i0), (q1, i1))):

            @pl.when(pl.program_id(0) == b)
            def _(qb=qb, ib=ib):
                final_kernel(qb, ib, run, state, out)

    whole = pl.BlockSpec((BLK, width), lambda b: (0, 0))
    return pl.pallas_call(
        body,
        grid=(2,),
        in_specs=[
            whole,
            whole,
            whole,
            whole,
            pl.BlockSpec((BLK, 4), lambda b: (b, 0)),
            pl.BlockSpec((1, 4, HEAD, HEAD), lambda b: (b, 0, 0, 0)),
        ],
        out_specs=pl.BlockSpec((BLK, width), lambda b: (b, 0)),
        out_shape=jax.ShapeDtypeStruct((rows, width), BF16),
        compiler_params=params(),
        cost_estimate=pl.CostEstimate(
            flops=4 * rows * width * HEAD, bytes_accessed=5 * 2**20, transcendentals=rows * 8
        ),
        name="finish",
    )(*q, *intra, run, states)


def ring(n, by):
    return [(i, (i + by) % n) for i in range(n)]


def gather_tokens(tokens):
    n = lax.axis_size("fsdp")
    ahead = functools.partial(lax.ppermute, axis_name="fsdp", perm=ring(n, 1))
    back = functools.partial(lax.ppermute, axis_name="fsdp", perm=ring(n, -1))
    top, bottom = tokens[:BLK], tokens[BLK:]
    left0, right1 = ahead(top), back(bottom)
    left1, right0 = ahead(bottom), back(top)
    far0, far1 = ahead(left0), back(right1)
    return (top, left0, right0, far0), (bottom, left1, right1, far1)


def entering(state, whole):
    n = lax.axis_size("seq")
    place = lax.axis_index("seq")
    heads = whole.shape[1]
    at = jnp.arange(n)
    between = (at[None, None, :] > at[None, :, None]) & (at[None, None, :] < at[:, None, None])
    head = place * heads // n
    mine = lax.dynamic_index_in_dim(whole, head, 1, False)
    gap = jnp.sum(jnp.where(between, mine[None, None, :], 0.0), axis=2)
    factor = jnp.where(at[:, None] > at[None, :], jnp.exp(gap), 0.0)
    piece = lax.all_to_all(state.reshape(n, -1, HEAD), "seq", 0, 0, tiled=True)
    prefix = jnp.dot(factor, piece.reshape(n, -1), precision=EXACT)
    back = lax.all_to_all(prefix.reshape(piece.shape), "seq", 0, 0, tiled=True)
    return back.reshape(state.shape)


def on_device(tokens, projection, log_decay):
    heads = log_decay.shape[1]
    x = lax.axis_index("fsdp")
    order = jnp.remainder(x + jnp.array([0, 3, 1, 2], jnp.int32), 4).astype(jnp.int32)
    first, second = gather_tokens(tokens)
    kv_weights = lax.all_gather(projection[1:], "seq", axis=1, tiled=True)
    q_weights = lax.all_gather(projection[:1], "seq", axis=1, tiled=True)

    decay = log_decay.reshape(2, BLK, heads)
    lower = (jnp.arange(BLK)[:, None] >= jnp.arange(BLK)[None, :]).astype(F32)
    run = jnp.einsum("ts,bsh->bth", lower, decay, precision=EXACT)
    across = run.transpose(0, 2, 1)
    last = run[:, -1]
    whole = lax.all_gather(last[0] + last[1], "seq")

    k0, v0, fresh0 = project_kv(0, order, first, kv_weights, run[0], last[:1])
    k1, v1, fresh1 = project_kv(0, order, second, kv_weights, run[1], last[1:])
    kept = jnp.exp(last[1])[:, None, None]
    entry = entering(kept * fresh0 + fresh1, whole)
    q0, intra0 = project_q(0, order, first, q_weights, run[0], across[0], k0, v0)
    q1, intra1 = project_q(0, order, second, q_weights, run[1], across[1], k1, v1)
    states = jnp.stack([entry, jnp.exp(last[0])[:, None, None] * entry + fresh0])
    return finish((q0, q1), (intra0, intra1), run.reshape(2 * BLK, heads), states)


def solution(mesh):
    in_specs = (P("seq", "fsdp"), P(None, "seq", "fsdp"), P("seq", "fsdp"))
    out_specs = P("seq", "fsdp")
    return jax.shard_map(
        on_device, mesh=mesh, in_specs=in_specs, out_specs=out_specs, check_vma=False
    )
```

time: 449 us -> 210 us (0.47)
  the two profiles are of different devices: /device:TPU:249 before, /device:TPU:1 now
where the time goes in v1:
time: 210 us
  waiting for transfers between devices  73.7 us (35%)
  Pallas kernels  45 us (21%)
  blocking collectives  43 us (20%)
  starting transfers between devices  21.1 us (10%)
  between operations  13.6 us (6%)
  local copies, waits for them, and re-layouts  8.9 us (4%)
  other arithmetic  3.79 us (2%)
    all_gather x1, blocking collectives, on_device(): whole = lax.all_gather(last[0] + last[1], 'seq')  43 us
    all_gather x1, waiting for transfers between devices, on_device(): kv_weights = lax.all_gather(projection[1:], 'seq', axis=1, tiled=True)  37.7 us
    pallas_call x2, Pallas kernels, project_kv(): pl.pallas_call(kv_kernel, grid_spec=pltpu.PrefetchScalarGridSpec(num_scal...  21.4 us
    ppermute x2, waiting for transfers between devices, gather_tokens(): left0, right1 = (ahead(top), back(bottom))  19.2 us
    pallas_call x2, Pallas kernels, project_q(): pl.pallas_call(q_kernel, grid_spec=pltpu.PrefetchScalarGridSpec(num_scala...  19 us
    ppermute x2, waiting for transfers between devices, gather_tokens(): left1, right0 = (ahead(bottom), back(top))  16.5 us
    all_to_all x1, starting transfers between devices, entering(): piece = lax.all_to_all(state.reshape(n, -1, HEAD), 'seq', 0, 0, tiled=True)  6.08 us
    all_to_all x1, starting transfers between devices, entering(): back = lax.all_to_all(prefix.reshape(piece.shape), 'seq', 0, 0, tiled=True)  5.34 us
  transfers between devices with their start and end apart: 10, of which 4 were waited for; matrix products, arithmetic and copies ran while one was open for 5% of the time, Pallas kernels for 19%

profile of v1, /device:TPU:1, one launch (start us, length us, event | category | flops | bytes accessed | tf_op | source)
XLA Modules:
  0.0 209.8 jit_solution(13625983361771005440)
XLA Ops:
  6.5 0.0 copy-start
  6.5 0.0 all-gather.6.cloned.1.call-start
  6.5 1.6 slice.49
  8.1 0.0 all-gather.6.cloned.1.call-update
  8.1 0.0 all-gather.4.cloned.1.call-start
  8.2 1.5 slice.46
  9.6 0.0 all-gather.4.cloned.1.call-update
  9.7 0.0 copy-start.5
  9.7 1.7 fusion.14
  11.4 0.0 copy-start.2
  11.4 0.0 copy-start.3
  11.4 2.1 %collective-permute-start = (bf16[512,1024]{1,0:T(8,128)(2,1)S(1)}, bf16[512,1024]{1,0:T(8,128)(2,1)}, u32[]{:S(2)}, u32[]{:S(2)}) collective-permute-start(bf16[512,1024]{1,0:T(8,128)(2,1)S(1)} %get-tuple-element.26.own), channel_id=1, source_target_pairs={{0,1},{1,2},{2,3},{3,0},{4,5},{5,6},{6,7},{7,4},{8,9},{9,10},{10,1... | collective-permute-start | bytes 3145736 | tf_op jit(solution)/shard_map/ppermute | solution.py:208
  13.5 1.4 collective-permute-start.4
  14.9 1.4 collective-permute-start.1
  16.3 19.2 %collective-permute-done.left = bf16[512,1024]{1,0:T(8,128)(2,1)} collective-permute-done((bf16[512,1024]{1,0:T(8,128)(2,1)S(1)}, bf16[512,1024]{1,0:T(8,128)(2,1)}, u32[]{:S(2)}, u32[]{:S(2)}) %collective-permute-start) | collective-permute-done | bytes 1048608 | tf_op jit(solution)/shard_map/ppermute | solution.py:208
  35.5 1.9 collective-permute-start.2
  37.4 1.5 collective-permute-start.3
  38.9 0.0 copy-done
  38.9 0.4 fusion.1
  39.3 0.3 copy.19
  39.6 0.0 copy-start.1
  39.6 0.0 collective-permute-done.4.right
  39.6 1.4 collective-permute-start.5
  41.1 0.0 copy-done.5
  41.1 0.5 and_select_fusion.order
  41.5 0.6 exponential_bitcast_fusion
  42.1 0.8 slice_bitcast_fusion
  42.9 16.5 %collective-permute-done.1.right = bf16[512,1024]{1,0:T(8,128)(2,1)} collective-permute-done((bf16[512,1024]{1,0:T(8,128)(2,1)S(1)}, bf16[512,1024]{1,0:T(8,128)(2,1)}, u32[]{:S(2)}, u32[]{:S(2)}) %collective-permute-start.1) | collective-permute-done | bytes 1048608 | tf_op jit(solution)/shard_map/ppermute | solution.py:209
  59.5 0.2 collective-permute-done.2.far
  59.7 37.7 %all-gather.6.cloned.1.call-done.weights = bf16[2,4096,512]{2,1,0:T(8,128)(2,1)} async-done(((bf16[2,64,512]{2,1,0:T(8,128)(2,1)}), bf16[2,4096,512]{2,1,0:T(8,128)(2,1)}) %all-gather.6.cloned.1.call-update) | async-done | bytes 8388624 | tf_op jit(solution)/shard_map/all_gather | solution.py:235
  97.4 0.0 copy-done.2
  97.4 10.6 %kv0.2 = (bf16[512,512]{1,0:T(8,128)(2,1)}, bf16[512,512]{1,0:T(8,128)(2,1)}, f32[4,128,128]{2,1,0:T(8,128)}) custom-call(s32[4]{0:T(128)} %and_select_fusion.order, bf16[512,1024]{1,0:T(8,128)(2,1)} %copy-done.2, bf16[512,1024]{1,0:T(8,128)(2,1)} %collective-permute-done.left, bf16[512,1024]{1,0:T(8,128)(2,1)} %collective-permute-done.1.right, ...), custom_call_target="tpu_custom_call" | custom-call | flops 4294967296 | bytes 14680064 | tf_op jit(solution)/shard_map/kv0/pallas_call | solution.py:109
  108.0 0.0 copy-done.3
  108.0 0.0 collective-permute-done.3.left
  108.0 0.0 collective-permute-done.5.far
  108.0 0.0 copy-start.4
  108.0 10.8 %kv0.3 = (bf16[512,512]{1,0:T(8,128)(2,1)}, bf16[512,512]{1,0:T(8,128)(2,1)}, f32[4,128,128]{2,1,0:T(8,128)}) custom-call(s32[4]{0:T(128)} %and_select_fusion.order, bf16[512,1024]{1,0:T(8,128)(2,1)} %copy-done.3, bf16[512,1024]{1,0:T(8,128)(2,1)} %collective-permute-done.3.left, bf16[512,1024]{1,0:T(8,128)(2,1)} %collective-permute-done.4.right, ...), custom_call_target="tpu_custom_call" | custom-call | flops 4294967296 | bytes 14680064 | tf_op jit(solution)/shard_map/kv0/pallas_call | solution.py:109
  118.8 0.0 copy-done.4
  118.8 1.7 multiply_add_fusion
  120.6 6.1 %all-to-all-start = ((f32[64,8,128]{2,1,0:T(8,128)}), f32[64,8,128]{2,1,0:T(8,128)S(1)}, u32[]{:S(2)}, u32[]{:S(2)}) async-start(f32[64,8,128]{2,1,0:T(8,128)} %bitcast.14), calls=%async_computation | async-start | bytes 524288 | tf_op jit(solution)/shard_map/all_to_all | solution.py:224
  126.7 0.0 copy-done.1
  126.7 43.0 %all-gather = f32[64,1,4]{2,1,0:T(1,128)S(1)} all-gather(f32[1,1,4]{2,1,0:T(1,128)S(1)} %add_bitcast_fusion), channel_id=1, replica_groups=mesh['seq'=64,'fsdp'=4] {'seq'}, dimensions={0}, use_global_device_ids=true | all-gather | bytes 1040 | tf_op jit(solution)/shard_map/all_gather | solution.py:243
  169.7 0.9 dynamic-slice_reduce_fusion
  170.6 0.6 select_reduce_fusion
  171.3 0.0 all-to-all-done
  171.3 0.4 fusion.3
  171.7 0.9 copy.21
  172.5 5.3 %all-to-all-start.1 = ((f32[64,8,128]{2,1,0:T(8,128)}), f32[64,8,128]{2,1,0:T(8,128)S(1)}, u32[]{:S(2)}, u32[]{:S(2)}) async-start(f32[64,8,128]{2,1,0:T(8,128)} %copy.21), calls=%async_computation.1 | async-start | bytes 524288 | tf_op jit(solution)/shard_map/all_to_all | solution.py:226
  177.9 0.6 slice_bitcast_fusion.2
  178.5 0.0 all-gather.4.cloned.1.call-done.weights
  178.5 9.5 %q0.3 = (bf16[512,512]{1,0:T(8,128)(2,1)}, f32[512,512]{1,0:T(8,128)}) custom-call(s32[4]{0:T(128)} %and_select_fusion.order, bf16[512,1024]{1,0:T(8,128)(2,1)} %copy-done.3, bf16[512,1024]{1,0:T(8,128)(2,1)} %collective-permute-done.3.left, bf16[512,1024]{1,0:T(8,128)(2,1)} %collective-permute-done.4.right, bf16[512,1024]{1,0:T(8,128)(2,1)} %collective-permute-done.5.far, ...), custom_call_target="tpu_custom_call" | custom-call | flops 2147483648 | bytes 10485760 | tf_op jit(solution)/shard_map/q0/pallas_call | solution.py:138
  188.0 9.5 %q0.2 = (bf16[512,512]{1,0:T(8,128)(2,1)}, f32[512,512]{1,0:T(8,128)}) custom-call(s32[4]{0:T(128)} %and_select_fusion.order, bf16[512,1024]{1,0:T(8,128)(2,1)} %copy-done.2, bf16[512,1024]{1,0:T(8,128)(2,1)} %collective-permute-done.left, bf16[512,1024]{1,0:T(8,128)(2,1)} %collective-permute-done.1.right, bf16[512,1024]{1,0:T(8,128)(2,1)} %collective-permute-done.2.far, ...), custom_call_target="tpu_custom_call" | custom-call | flops 2147483648 | bytes 10485760 | tf_op jit(solution)/shard_map/q0/pallas_call | solution.py:138
  197.5 0.0 all-to-all-done.1
  197.5 0.1 fusion.7
  197.6 0.8 pad_maximum_fusion.state
  198.4 4.6 %finish.1 = bf16[1024,512]{1,0:T(8,128)(2,1)} custom-call(bf16[512,512]{1,0:T(8,128)(2,1)} %get-tuple-element.17.q0, bf16[512,512]{1,0:T(8,128)(2,1)} %get-tuple-element.20.q1, f32[512,512]{1,0:T(8,128)} %get-tuple-element.21.i0, f32[512,512]{1,0:T(8,128)} %get-tuple-element.22.i1, f32[1024,4]{1,0:T(8,128)} %bitcast.62, f32[2,4,128,128]{3,2,1,0:T(8,128)} %pad_maximum_fusion.state), custom_call_target="tpu_custom_call" | custom-call | flops 268435456 | bytes 5242880 | tf_op jit(solution)/shard_map/finish/pallas_call | solution.py:178
  (2 shorter events, 0.0 us)
Async XLA Ops:
  6.5 32.4 %copy-start = (f32[1024,4]{0,1:T(4,128)S(1)}, f32[1024,4]{0,1:T(4,128)}, u32[]{:S(2)}) copy-start(f32[1024,4]{0,1:T(4,128)} %param.6) | copy-start | bytes 49156
  6.5 90.9 %all-gather.6.cloned.1.call-start = ((), (), s32[]{:S(2)}) async-start(), calls=%async_computation.3 | async-start | bytes 8519680 | tf_op jit(solution)/shard_map/all_gather | solution.py:235
  8.1 170.4 %all-gather.4.cloned.1.call-start = ((), (), s32[]{:S(2)}) async-start(), calls=%async_computation.2 | async-start | bytes 4259840 | tf_op jit(solution)/shard_map/all_gather | solution.py:236
  9.7 31.4 %copy-start.5 = (s32[4]{0:T(128)S(1)}, s32[4]{0:T(128)}, u32[]{:S(2)}) copy-start(s32[4]{0:T(128)} %constant.47.clone) | copy-start | bytes 52
  11.4 86.0 %copy-start.2 = (bf16[512,1024]{1,0:T(8,128)(2,1)}, bf16[512,1024]{1,0:T(8,128)(2,1)S(1)}, u32[]{:S(2)}) copy-start(bf16[512,1024]{1,0:T(8,128)(2,1)S(1)} %get-tuple-element.26.own) | copy-start | bytes 3145732
  11.4 96.6 %copy-start.3 = (bf16[512,1024]{1,0:T(8,128)(2,1)}, bf16[512,1024]{1,0:T(8,128)(2,1)S(1)}, u32[]{:S(2)}) copy-start(bf16[512,1024]{1,0:T(8,128)(2,1)S(1)} %get-tuple-element.25.own) | copy-start | bytes 3145732
  11.4 24.1 %collective-permute-start = (bf16[512,1024]{1,0:T(8,128)(2,1)S(1)}, bf16[512,1024]{1,0:T(8,128)(2,1)}, u32[]{:S(2)}, u32[]{:S(2)}) collective-permute-start(bf16[512,1024]{1,0:T(8,128)(2,1)S(1)} %get-tuple-element.26.own), channel_id=1, source_target_pairs={{0,1},{1,2},{2,3},{3,0},{4,5},{5,6},{6,7},{7,4},{8,9},{9,10},{10,1... | collective-permute-start | bytes 3145736 | tf_op jit(solution)/shard_map/ppermute | solution.py:208
  13.5 26.1 %collective-permute-start.4 = (bf16[512,1024]{1,0:T(8,128)(2,1)S(1)}, bf16[512,1024]{1,0:T(8,128)(2,1)}, u32[]{:S(2)}, u32[]{:S(2)}) collective-permute-start(bf16[512,1024]{1,0:T(8,128)(2,1)S(1)} %get-tuple-element.25.own), channel_id=1, source_target_pairs={{0,3},{1,0},{2,1},{3,2},{4,7},{5,4},{6,5},{7,6},{8,11},{9,8},{10,9... | collective-permute-start | bytes 3145736 | tf_op jit(solution)/shard_map/ppermute | solution.py:208
  14.9 44.6 %collective-permute-start.1 = (bf16[512,1024]{1,0:T(8,128)(2,1)S(1)}, bf16[512,1024]{1,0:T(8,128)(2,1)}, u32[]{:S(2)}, u32[]{:S(2)}) collective-permute-start(bf16[512,1024]{1,0:T(8,128)(2,1)S(1)} %get-tuple-element.26.own), channel_id=1, source_target_pairs={{0,3},{1,0},{2,1},{3,2},{4,7},{5,4},{6,5},{7,6},{8,11},{9,8},{10,9... | collective-permute-start | bytes 3145736 | tf_op jit(solution)/shard_map/ppermute | solution.py:209
  35.5 24.2 %collective-permute-start.2 = (bf16[512,1024]{1,0:T(8,128)(2,1)}, bf16[512,1024]{1,0:T(8,128)(2,1)}, u32[]{:S(2)}, u32[]{:S(2)}) collective-permute-start(bf16[512,1024]{1,0:T(8,128)(2,1)} %collective-permute-done.left), channel_id=1, source_target_pairs={{0,1},{1,2},{2,3},{3,0},{4,5},{5,6},{6,7},{7,4},{8,9},{9,10},{10,1... | collective-permute-start | bytes 3145736 | tf_op jit(solution)/shard_map/ppermute | solution.py:210
  37.4 70.6 %collective-permute-start.3 = (bf16[512,1024]{1,0:T(8,128)(2,1)S(1)}, bf16[512,1024]{1,0:T(8,128)(2,1)}, u32[]{:S(2)}, u32[]{:S(2)}) collective-permute-start(bf16[512,1024]{1,0:T(8,128)(2,1)S(1)} %get-tuple-element.25.own), channel_id=1, source_target_pairs={{0,1},{1,2},{2,3},{3,0},{4,5},{5,6},{6,7},{7,4},{8,9},{9,10},{10,1... | collective-permute-start | bytes 3145736 | tf_op jit(solution)/shard_map/ppermute | solution.py:209
  39.6 87.1 %copy-start.1 = (f32[512,2,4]{2,0,1:T(8,128)}, f32[512,2,4]{2,0,1:T(8,128)S(1)}, u32[]{:S(2)}) copy-start(f32[512,2,4]{2,0,1:T(8,128)S(1)} %copy.19) | copy-start | bytes 49156
  39.6 68.4 %collective-permute-start.5 = (bf16[512,1024]{1,0:T(8,128)(2,1)}, bf16[512,1024]{1,0:T(8,128)(2,1)}, u32[]{:S(2)}, u32[]{:S(2)}) collective-permute-start(bf16[512,1024]{1,0:T(8,128)(2,1)} %collective-permute-done.4.right), channel_id=1, source_target_pairs={{0,3},{1,0},{2,1},{3,2},{4,7},{5,4},{6,5},{7,6},{8,11},{9,8},{10,9... | collective-permute-start | bytes 3145736 | tf_op jit(solution)/shard_map/ppermute | solution.py:210
  108.0 10.8 %copy-start.4 = (f32[4,128,128]{2,1,0:T(8,128)S(1)}, f32[4,128,128]{2,1,0:T(8,128)}, u32[]{:S(2)}) copy-start(f32[4,128,128]{2,1,0:T(8,128)} %get-tuple-element.23) | copy-start | bytes 786436
  120.6 50.7 %all-to-all-start = ((f32[64,8,128]{2,1,0:T(8,128)}), f32[64,8,128]{2,1,0:T(8,128)S(1)}, u32[]{:S(2)}, u32[]{:S(2)}) async-start(f32[64,8,128]{2,1,0:T(8,128)} %bitcast.14), calls=%async_computation | async-start | bytes 524288 | tf_op jit(solution)/shard_map/all_to_all | solution.py:224
  172.5 25.0 %all-to-all-start.1 = ((f32[64,8,128]{2,1,0:T(8,128)}), f32[64,8,128]{2,1,0:T(8,128)S(1)}, u32[]{:S(2)}, u32[]{:S(2)}) async-start(f32[64,8,128]{2,1,0:T(8,128)} %copy.21), calls=%async_computation.1 | async-start | bytes 524288 | tf_op jit(solution)/shard_map/all_to_all | solution.py:226
Sparse Core Ops, SparseCore 0:
  10.2 87.1 all-gather.5
  100.2 76.3 all-gather.3

commit v2 on v0

v2 whole, which is shorter than its diff:
```python
import functools

import jax
import jax.numpy as jnp
from jax import lax
from jax.experimental import pallas as pl
from jax.experimental.pallas import tpu as pltpu
from jax.sharding import PartitionSpec as P

BLK = 512
HEAD = 128
DEPTH = 1024
X = 4
MIB = 2**20
F32 = jnp.float32
BF16 = jnp.bfloat16
EXACT = lax.Precision.HIGHEST
LEFT = pl.BlockSpec(memory_space=pl.ANY)
SCALARS = pl.BlockSpec(memory_space=pltpu.SMEM)


def silu(v):
    return v / (1.0 + jnp.exp(-v))


class Operands:
    def __init__(self, order, tokens, weights, matrices, token_slots, weight_slots, sems):
        self.token_slots, self.weight_slots = token_slots, weight_slots
        own, *rest = tokens
        self.pending = {}
        count = 0

        def add(key, src, dst):
            nonlocal count
            copy = pltpu.make_async_copy(src, dst, sems.at[count])
            copy.start()
            self.pending.setdefault(key, []).append(copy)
            count += 1

        def token(b):
            for d in range(X):
                src = own.at[pl.ds(b * BLK, BLK)] if d == 0 else rest[3 * b + d - 1]
                add(("t", b), src, token_slots.at[b, :, pl.ds(d * DEPTH, DEPTH)])

        def weight(m):
            for d in range(X):
                rows = pl.ds(pl.multiple_of(order[d] * DEPTH, DEPTH), DEPTH)
                add(("w", m), weights.at[matrices[m], rows], weight_slots.at[m, pl.ds(d * DEPTH, DEPTH)])

        weight(0)
        token(0)
        for m in range(1, len(matrices)):
            weight(m)
        token(1)

    def project(self, b, m):
        for key in (("t", b), ("w", m)):
            for copy in self.pending.pop(key, ()):
                copy.wait()
        return jnp.dot(self.token_slots[b], self.weight_slots[m], preferred_element_type=F32)


def kv_kernel(order, *refs):
    tokens, weights = refs[:7], refs[7]
    run, last, k_out, v_out, fresh, final, *scratch = refs[8:]
    operands = Operands(order, tokens, weights, (1, 2), *scratch)
    for b in range(2):
        rows = slice(b * BLK, (b + 1) * BLK)
        k = silu(operands.project(b, 0)).astype(BF16)
        k_out[rows] = k
        v = operands.project(b, 1).astype(BF16)
        v_out[rows] = v
        for h in range(4):
            cols = slice(h * HEAD, (h + 1) * HEAD)
            ends = last[b : b + 1, h : h + 1]
            fade = jnp.exp(ends - run[b, :, h : h + 1])
            carried = (k[:, cols].astype(F32) * fade).astype(BF16)
            new = lax.dot_general(
                carried, v[:, cols], (((0,), (0,)), ((), ())), preferred_element_type=F32
            )
            if b == 0:
                fresh[h] = new
            else:
                final[h] = jnp.exp(ends) * fresh[h] + new


def q_kernel(order, *refs):
    tokens, weights = refs[:7], refs[7]
    run, across, k, v, q_out, intra, *scratch = refs[8:]
    operands = Operands(order, tokens, weights, (0,), *scratch)
    half = BLK // 2
    for b in range(2):
        base = b * BLK
        q = silu(operands.project(b, 0)).astype(BF16)
        q_out[base : base + BLK] = q
        for h in range(4):
            cols = slice(h * HEAD, (h + 1) * HEAD)
            for t in range(2):
                rows = slice(t * half, (t + 1) * half)
                wide = (t + 1) * half
                scores = lax.dot_general(
                    q[rows, cols],
                    k[base : base + wide, cols],
                    (((1,), (1,)), ((), ())),
                    preferred_element_type=F32,
                )
                gap = run[b, rows, h : h + 1] - across[b, h : h + 1, :wide]
                at = lax.broadcasted_iota(jnp.int32, gap.shape, 0) + t * half
                lower = at >= lax.broadcasted_iota(jnp.int32, gap.shape, 1)
                fading = jnp.exp(jnp.where(lower, gap, -1e30))
                mix = (fading * scores).astype(BF16)
                intra[base + t * half : base + wide, cols] = jnp.dot(
                    mix, v[base : base + wide, cols], preferred_element_type=F32
                )


def finish_kernel(q, intra, run, last, entry, fresh, out):
    b = pl.program_id(0)
    for h in range(4):
        cols = slice(h * HEAD, (h + 1) * HEAD)
        later = jnp.exp(last[0:1, h : h + 1]) * entry[h] + fresh[h]
        state = jnp.where(b == 0, entry[h], later)
        high = state.astype(BF16)
        low = (state - high.astype(F32)).astype(BF16)
        queries = q[:, cols]
        inter = jnp.dot(queries, high, preferred_element_type=F32)
        inter += jnp.dot(queries, low, preferred_element_type=F32)
        mixed = intra[:, cols] + jnp.exp(run[0, :, h : h + 1]) * inter
        scale = lax.rsqrt(jnp.mean(mixed * mixed, axis=-1, keepdims=True) + 1e-06)
        out[:, cols] = (mixed * scale).astype(BF16)


def params():
    return pltpu.CompilerParams(vmem_limit_bytes=56 * MIB)


def sized(shape, dtype):
    return jax.ShapeDtypeStruct(shape, dtype)


def whole(*shape):
    return pl.BlockSpec(shape, lambda step: (0,) * len(shape))


def slots(matrices):
    return [
        pltpu.VMEM((2, BLK, X * DEPTH), BF16),
        pltpu.VMEM((matrices, X * DEPTH, 4 * HEAD), BF16),
        pltpu.SemaphoreType.DMA((8 + 4 * matrices,)),
    ]


def project_kv(order, tokens, weights, run, last):
    wide = 4 * HEAD
    return pl.pallas_call(
        kv_kernel,
        grid=(1,),
        in_specs=[SCALARS] + [LEFT] * 8 + [whole(2, BLK, 4), whole(2, 4)],
        out_specs=[whole(2 * BLK, wide)] * 2 + [whole(4, HEAD, HEAD)] * 2,
        out_shape=[sized((2 * BLK, wide), BF16)] * 2 + [sized((4, HEAD, HEAD), F32)] * 2,
        scratch_shapes=slots(2),
        compiler_params=params(),
        cost_estimate=pl.CostEstimate(
            flops=4 * BLK * 4096 * 1024, bytes_accessed=20 * MIB, transcendentals=MIB
        ),
        name="keys_values",
    )(order, *tokens, weights, run, last)


def project_q(order, tokens, weights, run, across, k, v):
    wide = 4 * HEAD
    return pl.pallas_call(
        q_kernel,
        grid=(1,),
        in_specs=[SCALARS]
        + [LEFT] * 8
        + [whole(2, BLK, 4), whole(2, 4, BLK)]
        + [whole(2 * BLK, wide)] * 2,
        out_specs=[whole(2 * BLK, wide)] * 2,
        out_shape=[sized((2 * BLK, wide), BF16), sized((2 * BLK, wide), F32)],
        scratch_shapes=slots(1),
        compiler_params=params(),
        cost_estimate=pl.CostEstimate(
            flops=4 * BLK * 4096 * 512, bytes_accessed=20 * MIB, transcendentals=2 * MIB
        ),
        name="queries",
    )(order, *tokens, weights, run, across, k, v)


def finish(q, intra, run, last, entry, fresh):
    block = pl.BlockSpec((BLK, 4 * HEAD), lambda b: (b, 0))
    return pl.pallas_call(
        finish_kernel,
        grid=(2,),
        in_specs=[
            block,
            block,
            pl.BlockSpec((1, BLK, 4), lambda b: (b, 0, 0)),
            whole(2, 4),
            whole(4, HEAD, HEAD),
            whole(4, HEAD, HEAD),
        ],
        out_specs=block,
        out_shape=sized((2 * BLK, 4 * HEAD), BF16),
        compiler_params=params(),
        cost_estimate=pl.CostEstimate(
            flops=8 * BLK * 512 * HEAD, bytes_accessed=5 * MIB, transcendentals=MIB // 64
        ),
        name="finish",
    )(q, intra, run, last, entry, fresh)


def ring(n, by):
    return [(i, (i + by) % n) for i in range(n)]


def gather_tokens(tokens):
    ahead = functools.partial(lax.ppermute, axis_name="fsdp", perm=ring(X, 1))
    back = functools.partial(lax.ppermute, axis_name="fsdp", perm=ring(X, -1))
    top, bottom = tokens[:BLK], tokens[BLK:]
    left0, right1 = ahead(top), back(bottom)
    left1, right0 = ahead(bottom), back(top)
    return left0, right0, ahead(left0), left1, right1, back(right1)


def factors(own, place):
    n = lax.axis_size("seq")
    heads = own.shape[0]
    row = jnp.pad(own, (0, HEAD - heads))
    whole = lax.all_to_all(jnp.broadcast_to(row, (n, 8, HEAD)), "seq", 0, 0, tiled=True)
    at = jnp.arange(n)
    between = (at[None, None, :] > at[None, :, None]) & (at[None, None, :] < at[:, None, None])
    slices = n // heads
    mine = lax.dynamic_index_in_dim(whole[:, 0, :heads], place // slices, 1, False)
    gap = jnp.sum(jnp.where(between, mine[None, None, :], 0.0), axis=2)
    return jnp.where(at[:, None] > at[None, :], jnp.exp(gap), 0.0)


def prefixes(state, factor):
    n = factor.shape[0]
    piece = lax.all_to_all(state.reshape(n, -1, HEAD), "seq", 0, 0, tiled=True)
    return jnp.dot(factor, piece.reshape(n, -1), precision=EXACT).reshape(piece.shape)


def on_device(tokens, projection, log_decay):
    heads = log_decay.shape[1]
    x, place = lax.axis_index("fsdp"), lax.axis_index("seq")
    order = ((x + jnp.array([0, 3, 1, 2])) % X).astype(jnp.int32)

    weights = lax.all_gather(projection, "seq", axis=1, tiled=True)
    moved = gather_tokens(tokens)
    all_tokens = (tokens, *moved)

    decay = log_decay.reshape(2, BLK, heads)
    lower = (jnp.arange(BLK)[:, None] >= jnp.arange(BLK)[None, :]).astype(F32)
    run = jnp.einsum("ts,bsh->bth", lower, decay, precision=EXACT)
    across = run.transpose(0, 2, 1)
    last = run[:, -1]
    factor = factors(last[0] + last[1], place)
    order, run, across, last, weights, factor = lax.optimization_barrier(
        (order, run, across, last, weights, factor)
    )

    k, v, fresh, final = project_kv(order, all_tokens, weights, run, last)
    prefix = prefixes(final, factor)
    q, intra = project_q(order, all_tokens, weights, run, across, k, v)
    entry = lax.all_to_all(prefix, "seq", 0, 0, tiled=True).reshape(final.shape)
    return finish(q, intra, run, last, entry, fresh)


def solution(mesh):
    in_specs = (P("seq", "fsdp"), P(None, "seq", "fsdp"), P("seq", "fsdp"))
    out_specs = P("seq", "fsdp")
    return jax.shard_map(
        on_device, mesh=mesh, in_specs=in_specs, out_specs=out_specs, check_vma=False
    )
```

time: 449 us -> 172 us (0.38)
  the two profiles are of different devices: /device:TPU:249 before, /device:TPU:1 now
where the time goes in v2:
time: 172 us; the launch traced here: 171 us
  waiting for transfers between devices  66.4 us (39%)
  Pallas kernels  34.1 us (20%)
  starting transfers between devices  30 us (17%)
  blocking collectives  17.9 us (10%)
  between operations  13.6 us (8%)
  local copies, waits for them, and re-layouts  7.33 us (4%)
    all_gather x1, waiting for transfers between devices, on_device(): weights = lax.all_gather(projection, 'seq', axis=1, tiled=True)  36.2 us
    ppermute x2, waiting for transfers between devices, gather_tokens(): left0, right1 = (ahead(top), back(bottom))  18.7 us
    all_to_all x1, blocking collectives, prefixes(): piece = lax.all_to_all(state.reshape(n, -1, HEAD), 'seq', 0, 0, tiled=True)  17.9 us
    pallas_call x1, Pallas kernels, project_kv(): pl.pallas_call(kv_kernel, grid=(1,), in_specs=[SCALARS] + [LEFT] * 8 + [w...  15.5 us
    all_to_all x1, starting transfers between devices, factors(): lax.all_to_all(jnp.broadcast_to(row, (n, 8, HEAD)), 'seq', 0, 0, tiled=True)  14.5 us
    pallas_call x1, Pallas kernels, project_q(): pl.pallas_call(q_kernel, grid=(1,), in_specs=[SCALARS] + [LEFT] * 8 + [wh...  14 us
    all_to_all x1, waiting for transfers between devices, factors(): lax.all_to_all(jnp.broadcast_to(row, (n, 8, HEAD)), 'seq', 0, 0, tiled=True)  10.8 us
    all_to_all x1, starting transfers between devices, on_device(): entry = lax.all_to_all(prefix, 'seq', 0, 0, tiled=True).reshape(final.shape)  6.04 us
  transfers between devices with their start and end apart: 9, of which 3 were waited for; matrix products, arithmetic and copies ran while one was open for 4% of the time, Pallas kernels for 8%

profile of v2, /device:TPU:1, one launch (start us, length us, event | category | flops | bytes accessed | tf_op | source)
XLA Modules:
  0.0 171.4 jit_solution(12170061141536991093)
XLA Ops:
  6.5 0.0 copy-start
  6.5 0.0 all-gather.2.cloned.1.call-start
  6.5 0.7 all-gather.2.cloned.1.call-update
  7.3 0.0 copy-start.6
  7.3 3.1 %fusion.9 = (bf16[512,1024]{1,0:T(8,128)(2,1)}, bf16[512,1024]{1,0:T(8,128)(2,1)}) fusion(bf16[1024,1024]{1,0:T(8,128)(2,1)} %refs_0_.3), kind=kLoop, calls=%fused_computation.20 | loop fusion | bytes 4194304 | tf_op jit(solution)/shard_map/slice | solution.py:220
  10.4 3.3 %collective-permute-start.4 = (bf16[512,1024]{1,0:T(8,128)(2,1)}, bf16[512,1024]{1,0:T(8,128)(2,1)S(1)}, u32[]{:S(2)}, u32[]{:S(2)}) collective-permute-start(bf16[512,1024]{1,0:T(8,128)(2,1)} %get-tuple-element.29), channel_id=1, source_target_pairs={{0,3},{1,0},{2,1},{3,2},{4,7},{5,4},{6,5},{7,6},{8,11},{9,8},{10,9... | collective-permute-start | bytes 3145736 | tf_op jit(solution)/shard_map/ppermute | solution.py:221
  13.7 0.0 collective-permute-start
  13.7 0.2 collective-permute-start.3
  13.9 2.5 %collective-permute-start.1 = (bf16[512,1024]{1,0:T(8,128)(2,1)}, bf16[512,1024]{1,0:T(8,128)(2,1)}, u32[]{:S(2)}, u32[]{:S(2)}) collective-permute-start(bf16[512,1024]{1,0:T(8,128)(2,1)} %get-tuple-element.30), channel_id=1, source_target_pairs={{0,3},{1,0},{2,1},{3,2},{4,7},{5,4},{6,5},{7,6},{8,11},{9,8},{10,9... | collective-permute-start | bytes 3145736 | tf_op jit(solution)/shard_map/ppermute | solution.py:222
  16.4 0.0 copy-done
  16.4 0.4 fusion.1
  16.8 0.0 copy-start.5
  16.8 0.3 copy.21
  17.1 0.0 copy-start.1
  17.1 18.7 %collective-permute-done.4.refs_5_ = bf16[512,1024]{1,0:T(8,128)(2,1)S(1)} collective-permute-done((bf16[512,1024]{1,0:T(8,128)(2,1)}, bf16[512,1024]{1,0:T(8,128)(2,1)S(1)}, u32[]{:S(2)}, u32[]{:S(2)}) %collective-permute-start.4) | collective-permute-done | bytes 1048608 | tf_op jit(solution)/shard_map/ppermute | solution.py:221
  35.8 0.0 copy-start.2
  35.8 3.4 %collective-permute-start.5 = (bf16[512,1024]{1,0:T(8,128)(2,1)S(1)}, bf16[512,1024]{1,0:T(8,128)(2,1)}, u32[]{:S(2)}, u32[]{:S(2)}) collective-permute-start(bf16[512,1024]{1,0:T(8,128)(2,1)S(1)} %collective-permute-done.4.refs_5_), channel_id=1, source_target_pairs={{0,3},{1,0},{2,1},{3,2},{4,7},{5,4},{6,5},{7,6},{8,11},{9,8},{10,9... | collective-permute-start | bytes 3145736 | tf_op jit(solution)/shard_map/ppermute | solution.py:223
  39.2 0.0 collective-permute-done.refs_1_
  39.2 0.0 copy-start.3
  39.2 0.0 collective-permute-start.2
  39.3 0.8 broadcast_in_dim.30
  40.0 14.5 %all-to-all-start = ((f32[64,8,128]{2,1,0:T(8,128)}), f32[64,8,128]{2,1,0:T(8,128)S(1)}, u32[]{:S(2)}, u32[]{:S(2)}) async-start(f32[64,8,128]{2,1,0:T(8,128)} %broadcast_in_dim.30), calls=%async_computation | async-start | bytes 524288 | tf_op jit(solution)/shard_map/all_to_all | solution.py:230
  54.6 0.6 slice.28
  55.2 0.0 copy-done.6
  55.2 0.6 and_select_fusion.order
  55.8 10.8 %all-to-all-done = f32[64,8,128]{2,1,0:T(8,128)S(1)} async-done(((f32[64,8,128]{2,1,0:T(8,128)}), f32[64,8,128]{2,1,0:T(8,128)S(1)}, u32[]{:S(2)}, u32[]{:S(2)}) %all-to-all-start) | async-done | bytes 262176 | tf_op jit(solution)/shard_map/all_to_all | solution.py:230
  66.6 0.9 dynamic-slice_reduce_fusion
  67.6 0.6 select_reduce_fusion
  68.2 36.2 %all-gather.2.cloned.1.call-done.refs_7_ = bf16[3,4096,512]{2,1,0:T(8,128)(2,1)} async-done(((bf16[3,64,512]{2,1,0:T(8,128)(2,1)}), bf16[3,4096,512]{2,1,0:T(8,128)(2,1)}) %all-gather.2.cloned.1.call-update) | async-done | bytes 12582928 | tf_op jit(solution)/shard_map/all_gather | solution.py:250
  104.4 0.0 collective-permute-done.3.refs_4_
  104.4 0.0 collective-permute-done.1.refs_2_
  104.4 0.0 collective-permute-done.5.refs_6_
  104.4 0.0 collective-permute-done.2.refs_3_
  104.4 0.0 copy-done.1
  104.4 0.0 copy-done.2
  104.4 0.0 copy-done.3
  104.4 15.5 %keys_values.1 = (bf16[1024,512]{1,0:T(8,128)(2,1)}, bf16[1024,512]{1,0:T(8,128)(2,1)}, f32[4,128,128]{2,1,0:T(8,128)}, f32[4,128,128]{2,1,0:T(8,128)}) custom-call(s32[4]{0:T(128)} %and_select_fusion.order, bf16[1024,1024]{1,0:T(8,128)(2,1)} %refs_0_.3, bf16[512,1024]{1,0:T(8,128)(2,1)} %copy-done.3, bf16[512,1024]{1,0:T(8,128)(2,1)} %collective-permute-done.1.refs_2_, ...), custom_call_target="tpu_custom_call" | custom-call | flops 8589934592 | bytes 20971520 | tf_op jit(solution)/shard_map/keys_values/pallas_call | solution.py:155
  120.0 0.0 copy-done.5
  120.0 17.9 %all_to_all.15 = f32[64,8,128]{2,1,0:T(8,128)S(1)} all-to-all(f32[64,8,128]{2,1,0:T(8,128)} %bitcast.36), channel_id=1, replica_groups=mesh['seq'=64,'fsdp'=4] {'seq'}, dimensions={0} | all-to-all | bytes 524288 | tf_op jit(solution)/shard_map/all_to_all | solution.py:241
  137.9 0.4 fusion.3
  138.3 0.9 copy.23
  139.2 6.0 %all-to-all-start.2 = ((f32[64,8,128]{2,1,0:T(8,128)}), f32[64,8,128]{2,1,0:T(8,128)S(1)}, u32[]{:S(2)}, u32[]{:S(2)}) async-start(f32[64,8,128]{2,1,0:T(8,128)} %copy.23), calls=%async_computation.2 | async-start | bytes 524288 | tf_op jit(solution)/shard_map/all_to_all | solution.py:267
  145.2 14.0 %queries.1 = (bf16[1024,512]{1,0:T(8,128)(2,1)}, f32[1024,512]{1,0:T(8,128)}) custom-call(s32[4]{0:T(128)} %and_select_fusion.order, bf16[1024,1024]{1,0:T(8,128)(2,1)} %refs_0_.3, bf16[512,1024]{1,0:T(8,128)(2,1)} %copy-done.3, bf16[512,1024]{1,0:T(8,128)(2,1)} %collective-permute-done.1.refs_2_, bf16[512,1024]{1,0:T(8,128)(2,1)} %collective-permute-done.2.refs_3_, ...), custom_call_target="tpu_custom_call" | custom-call | flops 4294967296 | bytes 20971520 | tf_op jit(solution)/shard_map/queries/pallas_call | solution.py:172
  159.2 0.0 all-to-all-done.2
  159.2 0.0 copy-start.4
  159.3 0.7 copy-done.4
  160.0 4.5 %finish.1 = bf16[1024,512]{1,0:T(8,128)(2,1)} custom-call(bf16[1024,512]{1,0:T(8,128)(2,1)} %get-tuple-element.24.q, f32[1024,512]{1,0:T(8,128)} %get-tuple-element.25.intra, f32[2,512,4]{2,1,0:T(8,128)} %bitcast.33, f32[2,4]{1,0:T(2,128)} %bitcast.39, f32[4,128,128]{2,1,0:T(8,128)} %bitcast.34, f32[4,128,128]{2,1,0:T(8,128)} %get-tuple-element.28.fresh), custom_call_target="tpu_custom_call" | custom-call | flops 268435456 | bytes 5242880 | tf_op jit(solution)/shard_map/finish/pallas_call | solution.py:192
  (5 shorter events, 0.1 us)
Async XLA Ops:
  6.5 9.8 %copy-start = (f32[1024,4]{0,1:T(4,128)S(1)}, f32[1024,4]{0,1:T(4,128)}, u32[]{:S(2)}) copy-start(f32[1024,4]{0,1:T(4,128)} %param.6) | copy-start | bytes 49156
  6.5 97.8 %all-gather.2.cloned.1.call-start = ((), (), s32[]{:S(2)}) async-start(), calls=%async_computation.3 | async-start | bytes 12779520 | tf_op jit(solution)/shard_map/all_gather | solution.py:250
  7.3 48.0 %copy-start.6 = (s32[4]{0:T(128)S(1)}, s32[4]{0:T(128)}, u32[]{:S(2)}) copy-start(s32[4]{0:T(128)} %constant.49.clone) | copy-start | bytes 52
  10.4 25.5 %collective-permute-start.4 = (bf16[512,1024]{1,0:T(8,128)(2,1)}, bf16[512,1024]{1,0:T(8,128)(2,1)S(1)}, u32[]{:S(2)}, u32[]{:S(2)}) collective-permute-start(bf16[512,1024]{1,0:T(8,128)(2,1)} %get-tuple-element.29), channel_id=1, source_target_pairs={{0,3},{1,0},{2,1},{3,2},{4,7},{5,4},{6,5},{7,6},{8,11},{9,8},{10,9... | collective-permute-start | bytes 3145736 | tf_op jit(solution)/shard_map/ppermute | solution.py:221
  13.7 25.6 %collective-permute-start = (bf16[512,1024]{1,0:T(8,128)(2,1)}, bf16[512,1024]{1,0:T(8,128)(2,1)S(1)}, u32[]{:S(2)}, u32[]{:S(2)}) collective-permute-start(bf16[512,1024]{1,0:T(8,128)(2,1)} %get-tuple-element.30), channel_id=1, source_target_pairs={{0,1},{1,2},{2,3},{3,0},{4,5},{5,6},{6,7},{7,4},{8,9},{9,10},{10,1... | collective-permute-start | bytes 3145736 | tf_op jit(solution)/shard_map/ppermute | solution.py:221
  13.7 90.7 %collective-permute-start.3 = (bf16[512,1024]{1,0:T(8,128)(2,1)}, bf16[512,1024]{1,0:T(8,128)(2,1)}, u32[]{:S(2)}, u32[]{:S(2)}) collective-permute-start(bf16[512,1024]{1,0:T(8,128)(2,1)} %get-tuple-element.29), channel_id=1, source_target_pairs={{0,1},{1,2},{2,3},{3,0},{4,5},{5,6},{6,7},{7,4},{8,9},{9,10},{10,1... | collective-permute-start | bytes 3145736 | tf_op jit(solution)/shard_map/ppermute | solution.py:222
  13.9 90.5 %collective-permute-start.1 = (bf16[512,1024]{1,0:T(8,128)(2,1)}, bf16[512,1024]{1,0:T(8,128)(2,1)}, u32[]{:S(2)}, u32[]{:S(2)}) collective-permute-start(bf16[512,1024]{1,0:T(8,128)(2,1)} %get-tuple-element.30), channel_id=1, source_target_pairs={{0,3},{1,0},{2,1},{3,2},{4,7},{5,4},{6,5},{7,6},{8,11},{9,8},{10,9... | collective-permute-start | bytes 3145736 | tf_op jit(solution)/shard_map/ppermute | solution.py:222
  16.8 103.2 %copy-start.5 = (f32[512,2,4]{0,2,1:T(4,128)}, f32[512,2,4]{0,2,1:T(4,128)S(1)}, u32[]{:S(2)}) copy-start(f32[512,2,4]{0,2,1:T(4,128)S(1)} %fusion.1) | copy-start | bytes 49156
  17.1 87.3 %copy-start.1 = (f32[512,2,4]{2,0,1:T(8,128)}, f32[512,2,4]{2,0,1:T(8,128)S(1)}, u32[]{:S(2)}) copy-start(f32[512,2,4]{2,0,1:T(8,128)S(1)} %copy.21) | copy-start | bytes 49156
  35.8 68.6 %copy-start.2 = (bf16[512,1024]{1,0:T(8,128)(2,1)}, bf16[512,1024]{1,0:T(8,128)(2,1)S(1)}, u32[]{:S(2)}) copy-start(bf16[512,1024]{1,0:T(8,128)(2,1)S(1)} %collective-permute-done.4.refs_5_) | copy-start | bytes 3145732
  35.8 68.6 %collective-permute-start.5 = (bf16[512,1024]{1,0:T(8,128)(2,1)S(1)}, bf16[512,1024]{1,0:T(8,128)(2,1)}, u32[]{:S(2)}, u32[]{:S(2)}) collective-permute-start(bf16[512,1024]{1,0:T(8,128)(2,1)S(1)} %collective-permute-done.4.refs_5_), channel_id=1, source_target_pairs={{0,3},{1,0},{2,1},{3,2},{4,7},{5,4},{6,5},{7,6},{8,11},{9,8},{10,9... | collective-permute-start | bytes 3145736 | tf_op jit(solution)/shard_map/ppermute | solution.py:223
  39.2 65.2 %copy-start.3 = (bf16[512,1024]{1,0:T(8,128)(2,1)}, bf16[512,1024]{1,0:T(8,128)(2,1)S(1)}, u32[]{:S(2)}) copy-start(bf16[512,1024]{1,0:T(8,128)(2,1)S(1)} %collective-permute-done.refs_1_) | copy-start | bytes 3145732
  39.2 65.2 %collective-permute-start.2 = (bf16[512,1024]{1,0:T(8,128)(2,1)S(1)}, bf16[512,1024]{1,0:T(8,128)(2,1)}, u32[]{:S(2)}, u32[]{:S(2)}) collective-permute-start(bf16[512,1024]{1,0:T(8,128)(2,1)S(1)} %collective-permute-done.refs_1_), channel_id=1, source_target_pairs={{0,1},{1,2},{2,3},{3,0},{4,5},{5,6},{6,7},{7,4},{8,9},{9,10},{10,1... | collective-permute-start | bytes 3145736 | tf_op jit(solution)/shard_map/ppermute | solution.py:223
  40.0 26.5 %all-to-all-start = ((f32[64,8,128]{2,1,0:T(8,128)}), f32[64,8,128]{2,1,0:T(8,128)S(1)}, u32[]{:S(2)}, u32[]{:S(2)}) async-start(f32[64,8,128]{2,1,0:T(8,128)} %broadcast_in_dim.30), calls=%async_computation | async-start | bytes 524288 | tf_op jit(solution)/shard_map/all_to_all | solution.py:230
  139.2 20.1 %all-to-all-start.2 = ((f32[64,8,128]{2,1,0:T(8,128)}), f32[64,8,128]{2,1,0:T(8,128)S(1)}, u32[]{:S(2)}, u32[]{:S(2)}) async-start(f32[64,8,128]{2,1,0:T(8,128)} %copy.23), calls=%async_computation.2 | async-start | bytes 524288 | tf_op jit(solution)/shard_map/all_to_all | solution.py:267
  159.2 0.7 copy-start.4
Sparse Core Ops, SparseCore 0:
  10.2 94.1 all-gather.1

commit v3 on v2

--- a/solution.py
+++ b/solution.py
@@ -81,7 +81,7 @@
             if b == 0:
                 fresh[h] = new
             else:
-                final[h] = jnp.exp(ends) * fresh[h] + new
+                final[h] = (jnp.exp(ends) * fresh[h] + new).astype(BF16)
 
 
 def q_kernel(order, *refs):
@@ -118,13 +118,10 @@
     b = pl.program_id(0)
     for h in range(4):
         cols = slice(h * HEAD, (h + 1) * HEAD)
-        later = jnp.exp(last[0:1, h : h + 1]) * entry[h] + fresh[h]
-        state = jnp.where(b == 0, entry[h], later)
-        high = state.astype(BF16)
-        low = (state - high.astype(F32)).astype(BF16)
-        queries = q[:, cols]
-        inter = jnp.dot(queries, high, preferred_element_type=F32)
-        inter += jnp.dot(queries, low, preferred_element_type=F32)
+        state = entry[h].astype(F32)
+        later = jnp.exp(last[0:1, h : h + 1]) * state + fresh[h]
+        state = jnp.where(b == 0, state, later).astype(BF16)
+        inter = jnp.dot(q[:, cols], state, preferred_element_type=F32)
         mixed = intra[:, cols] + jnp.exp(run[0, :, h : h + 1]) * inter
         scale = lax.rsqrt(jnp.mean(mixed * mixed, axis=-1, keepdims=True) + 1e-06)
         out[:, cols] = (mixed * scale).astype(BF16)
@@ -157,7 +154,8 @@
         grid=(1,),
         in_specs=[SCALARS] + [LEFT] * 8 + [whole(2, BLK, 4), whole(2, 4)],
         out_specs=[whole(2 * BLK, wide)] * 2 + [whole(4, HEAD, HEAD)] * 2,
-        out_shape=[sized((2 * BLK, wide), BF16)] * 2 + [sized((4, HEAD, HEAD), F32)] * 2,
+        out_shape=[sized((2 * BLK, wide), BF16)] * 2
+        + [sized((4, HEAD, HEAD), F32), sized((4, HEAD, HEAD), BF16)],
         scratch_shapes=slots(2),
         compiler_params=params(),
         cost_estimate=pl.CostEstimate(
@@ -239,7 +237,8 @@
 def prefixes(state, factor):
     n = factor.shape[0]
     piece = lax.all_to_all(state.reshape(n, -1, HEAD), "seq", 0, 0, tiled=True)
-    return jnp.dot(factor, piece.reshape(n, -1), precision=EXACT).reshape(piece.shape)
+    prefix = jnp.dot(factor, piece.astype(F32).reshape(n, -1), precision=EXACT)
+    return prefix.astype(BF16).reshape(piece.shape)
 
 
 def on_device(tokens, projection, log_decay):

time: 172 us -> 169 us (0.983)
  no operation moved by 1% of the time
where the time goes in v3:
time: 169 us; the launch traced here: 168 us
  waiting for transfers between devices  66.5 us (39%)
  Pallas kernels  34.2 us (20%)
  starting transfers between devices  28.9 us (17%)
  blocking collectives  16.3 us (10%)
  between operations  13.6 us (8%)
  local copies, waits for them, and re-layouts  7.1 us (4%)
    all_gather x1, waiting for transfers between devices, on_device(): weights = lax.all_gather(projection, 'seq', axis=1, tiled=True)  36.2 us
    ppermute x2, waiting for transfers between devices, gather_tokens(): left0, right1 = (ahead(top), back(bottom))  18.7 us
    all_to_all x1, blocking collectives, prefixes(): piece = lax.all_to_all(state.reshape(n, -1, HEAD), 'seq', 0, 0, tiled=True)  16.3 us
    pallas_call x1, Pallas kernels, project_kv(): pl.pallas_call(kv_kernel, grid=(1,), in_specs=[SCALARS] + [LEFT] * 8 + [w...  15.5 us
    all_to_all x1, starting transfers between devices, factors(): lax.all_to_all(jnp.broadcast_to(row, (n, 8, HEAD)), 'seq', 0, 0, tiled=True)  14.5 us
    pallas_call x1, Pallas kernels, project_q(): pl.pallas_call(q_kernel, grid=(1,), in_specs=[SCALARS] + [LEFT] * 8 + [wh...  14 us
    all_to_all x1, waiting for transfers between devices, factors(): lax.all_to_all(jnp.broadcast_to(row, (n, 8, HEAD)), 'seq', 0, 0, tiled=True)  10.9 us
    all_to_all x1, starting transfers between devices, on_device(): entry = lax.all_to_all(prefix, 'seq', 0, 0, tiled=True).reshape(final.shape)  4.89 us
  transfers between devices with their start and end apart: 9, of which 3 were waited for; matrix products, arithmetic and copies ran while one was open for 4% of the time, Pallas kernels for 8%

profile of v3, /device:TPU:1, one launch (start us, length us, event | category | flops | bytes accessed | tf_op | source)
XLA Modules:
  0.0 168.3 jit_solution(9547355006758063565)
XLA Ops:
  6.5 0.0 copy-start
  6.5 0.0 all-gather.2.cloned.1.call-start
  6.5 0.7 all-gather.2.cloned.1.call-update
  7.3 0.0 copy-start.6
  7.3 3.1 %fusion.8 = (bf16[512,1024]{1,0:T(8,128)(2,1)}, bf16[512,1024]{1,0:T(8,128)(2,1)}) fusion(bf16[1024,1024]{1,0:T(8,128)(2,1)} %refs_0_.3), kind=kLoop, calls=%fused_computation.19 | loop fusion | bytes 4194304 | tf_op jit(solution)/shard_map/slice | solution.py:218
  10.4 3.3 %collective-permute-start.4 = (bf16[512,1024]{1,0:T(8,128)(2,1)}, bf16[512,1024]{1,0:T(8,128)(2,1)S(1)}, u32[]{:S(2)}, u32[]{:S(2)}) collective-permute-start(bf16[512,1024]{1,0:T(8,128)(2,1)} %get-tuple-element.29), channel_id=1, source_target_pairs={{0,3},{1,0},{2,1},{3,2},{4,7},{5,4},{6,5},{7,6},{8,11},{9,8},{10,9... | collective-permute-start | bytes 3145736 | tf_op jit(solution)/shard_map/ppermute | solution.py:219
  13.7 0.0 collective-permute-start
  13.7 0.2 collective-permute-start.3
  13.9 2.5 %collective-permute-start.1 = (bf16[512,1024]{1,0:T(8,128)(2,1)}, bf16[512,1024]{1,0:T(8,128)(2,1)}, u32[]{:S(2)}, u32[]{:S(2)}) collective-permute-start(bf16[512,1024]{1,0:T(8,128)(2,1)} %get-tuple-element.30), channel_id=1, source_target_pairs={{0,3},{1,0},{2,1},{3,2},{4,7},{5,4},{6,5},{7,6},{8,11},{9,8},{10,9... | collective-permute-start | bytes 3145736 | tf_op jit(solution)/shard_map/ppermute | solution.py:220
  16.4 0.0 copy-done
  16.4 0.4 fusion.2
  16.8 0.0 copy-start.5
  16.8 0.3 copy.12
  17.1 0.0 copy-start.1
  17.1 18.7 %collective-permute-done.4.refs_5_ = bf16[512,1024]{1,0:T(8,128)(2,1)S(1)} collective-permute-done((bf16[512,1024]{1,0:T(8,128)(2,1)}, bf16[512,1024]{1,0:T(8,128)(2,1)S(1)}, u32[]{:S(2)}, u32[]{:S(2)}) %collective-permute-start.4) | collective-permute-done | bytes 1048608 | tf_op jit(solution)/shard_map/ppermute | solution.py:219
  35.8 0.0 copy-start.2
  35.8 3.4 %collective-permute-start.5 = (bf16[512,1024]{1,0:T(8,128)(2,1)S(1)}, bf16[512,1024]{1,0:T(8,128)(2,1)}, u32[]{:S(2)}, u32[]{:S(2)}) collective-permute-start(bf16[512,1024]{1,0:T(8,128)(2,1)S(1)} %collective-permute-done.4.refs_5_), channel_id=1, source_target_pairs={{0,3},{1,0},{2,1},{3,2},{4,7},{5,4},{6,5},{7,6},{8,11},{9,8},{10,9... | collective-permute-start | bytes 3145736 | tf_op jit(solution)/shard_map/ppermute | solution.py:221
  39.2 0.0 collective-permute-done.refs_1_
  39.2 0.0 copy-start.3
  39.2 0.0 collective-permute-start.2
  39.3 0.8 broadcast_in_dim.30
  40.0 14.5 %all-to-all-start = ((f32[64,8,128]{2,1,0:T(8,128)}), f32[64,8,128]{2,1,0:T(8,128)S(1)}, u32[]{:S(2)}, u32[]{:S(2)}) async-start(f32[64,8,128]{2,1,0:T(8,128)} %broadcast_in_dim.30), calls=%async_computation | async-start | bytes 524288 | tf_op jit(solution)/shard_map/all_to_all | solution.py:228
  54.6 0.6 slice.28
  55.2 0.0 copy-done.6
  55.2 0.5 and_select_fusion.order
  55.7 10.9 %all-to-all-done = f32[64,8,128]{2,1,0:T(8,128)S(1)} async-done(((f32[64,8,128]{2,1,0:T(8,128)}), f32[64,8,128]{2,1,0:T(8,128)S(1)}, u32[]{:S(2)}, u32[]{:S(2)}) %all-to-all-start) | async-done | bytes 262176 | tf_op jit(solution)/shard_map/all_to_all | solution.py:228
  66.6 0.9 dynamic-slice_reduce_fusion
  67.6 0.6 select_reduce_fusion
  68.2 36.2 %all-gather.2.cloned.1.call-done.refs_7_ = bf16[3,4096,512]{2,1,0:T(8,128)(2,1)} async-done(((bf16[3,64,512]{2,1,0:T(8,128)(2,1)}), bf16[3,4096,512]{2,1,0:T(8,128)(2,1)}) %all-gather.2.cloned.1.call-update) | async-done | bytes 12582928 | tf_op jit(solution)/shard_map/all_gather | solution.py:249
  104.4 0.0 collective-permute-done.3.refs_4_
  104.4 0.0 collective-permute-done.1.refs_2_
  104.4 0.0 collective-permute-done.5.refs_6_
  104.4 0.0 collective-permute-done.2.refs_3_
  104.4 0.0 copy-done.1
  104.4 0.0 copy-done.2
  104.4 0.0 copy-done.3
  104.4 15.5 %keys_values.1 = (bf16[1024,512]{1,0:T(8,128)(2,1)}, bf16[1024,512]{1,0:T(8,128)(2,1)}, f32[4,128,128]{2,1,0:T(8,128)}, bf16[4,128,128]{2,1,0:T(8,128)(2,1)}) custom-call(s32[4]{0:T(128)} %and_select_fusion.order, bf16[1024,1024]{1,0:T(8,128)(2,1)} %refs_0_.3, bf16[512,1024]{1,0:T(8,128)(2,1)} %copy-done.3, ...), custom_call_target="tpu_custom_call" | custom-call | flops 8589934592 | bytes 20971520 | tf_op jit(solution)/shard_map/keys_values/pallas_call | solution.py:152
  119.9 0.0 copy-done.5
  120.0 16.3 %all_to_all.15 = bf16[64,8,128]{2,1,0:T(8,128)(2,1)S(1)} all-to-all(bf16[64,8,128]{2,1,0:T(8,128)(2,1)} %bitcast.28), channel_id=1, replica_groups=mesh['seq'=64,'fsdp'=4] {'seq'}, dimensions={0} | all-to-all | bytes 262144 | tf_op jit(solution)/shard_map/all_to_all | solution.py:239
  136.2 0.2 fusion
  136.5 0.7 copy.14
  137.2 4.9 %all-to-all-start.2 = ((bf16[64,8,128]{2,1,0:T(8,128)(2,1)}), bf16[64,8,128]{2,1,0:T(8,128)(2,1)S(1)}, u32[]{:S(2)}, u32[]{:S(2)}) async-start(bf16[64,8,128]{2,1,0:T(8,128)(2,1)} %bitcast.11), calls=%async_computation.2 | async-start | bytes 262144 | tf_op jit(solution)/shard_map/all_to_all | solution.py:266
  142.1 14.0 %queries.1 = (bf16[1024,512]{1,0:T(8,128)(2,1)}, f32[1024,512]{1,0:T(8,128)}) custom-call(s32[4]{0:T(128)} %and_select_fusion.order, bf16[1024,1024]{1,0:T(8,128)(2,1)} %refs_0_.3, bf16[512,1024]{1,0:T(8,128)(2,1)} %copy-done.3, bf16[512,1024]{1,0:T(8,128)(2,1)} %collective-permute-done.1.refs_2_, bf16[512,1024]{1,0:T(8,128)(2,1)} %collective-permute-done.2.refs_3_, ...), custom_call_target="tpu_custom_call" | custom-call | flops 4294967296 | bytes 20971520 | tf_op jit(solution)/shard_map/queries/pallas_call | solution.py:170
  156.1 0.0 all-to-all-done.2
  156.1 0.0 copy-start.4
  156.1 0.7 copy-done.4
  156.8 4.7 %finish.1 = bf16[1024,512]{1,0:T(8,128)(2,1)} custom-call(bf16[1024,512]{1,0:T(8,128)(2,1)} %get-tuple-element.24.q, f32[1024,512]{1,0:T(8,128)} %get-tuple-element.25.intra, f32[2,512,4]{2,1,0:T(8,128)} %bitcast.25, f32[2,4]{1,0:T(2,128)} %bitcast.31, bf16[4,128,128]{2,1,0:T(8,128)(2,1)} %bitcast.26, f32[4,128,128]{2,1,0:T(8,128)} %get-tuple-element.28.fresh), custom_call_target="tpu_custom_call" | custom-call | flops 268435456 | bytes 5242880 | tf_op jit(solution)/shard_map/finish/pallas_call | solution.py:190
  (5 shorter events, 0.1 us)
Async XLA Ops:
  6.5 9.8 %copy-start = (f32[1024,4]{0,1:T(4,128)S(1)}, f32[1024,4]{0,1:T(4,128)}, u32[]{:S(2)}) copy-start(f32[1024,4]{0,1:T(4,128)} %param.6) | copy-start | bytes 49156
  6.5 97.8 %all-gather.2.cloned.1.call-start = ((), (), s32[]{:S(2)}) async-start(), calls=%async_computation.3 | async-start | bytes 12779520 | tf_op jit(solution)/shard_map/all_gather | solution.py:249
  7.3 48.0 %copy-start.6 = (s32[4]{0:T(128)S(1)}, s32[4]{0:T(128)}, u32[]{:S(2)}) copy-start(s32[4]{0:T(128)} %constant.49.clone) | copy-start | bytes 52
  10.4 25.5 %collective-permute-start.4 = (bf16[512,1024]{1,0:T(8,128)(2,1)}, bf16[512,1024]{1,0:T(8,128)(2,1)S(1)}, u32[]{:S(2)}, u32[]{:S(2)}) collective-permute-start(bf16[512,1024]{1,0:T(8,128)(2,1)} %get-tuple-element.29), channel_id=1, source_target_pairs={{0,3},{1,0},{2,1},{3,2},{4,7},{5,4},{6,5},{7,6},{8,11},{9,8},{10,9... | collective-permute-start | bytes 3145736 | tf_op jit(solution)/shard_map/ppermute | solution.py:219
  13.7 25.6 %collective-permute-start = (bf16[512,1024]{1,0:T(8,128)(2,1)}, bf16[512,1024]{1,0:T(8,128)(2,1)S(1)}, u32[]{:S(2)}, u32[]{:S(2)}) collective-permute-start(bf16[512,1024]{1,0:T(8,128)(2,1)} %get-tuple-element.30), channel_id=1, source_target_pairs={{0,1},{1,2},{2,3},{3,0},{4,5},{5,6},{6,7},{7,4},{8,9},{9,10},{10,1... | collective-permute-start | bytes 3145736 | tf_op jit(solution)/shard_map/ppermute | solution.py:219
  13.7 90.7 %collective-permute-start.3 = (bf16[512,1024]{1,0:T(8,128)(2,1)}, bf16[512,1024]{1,0:T(8,128)(2,1)}, u32[]{:S(2)}, u32[]{:S(2)}) collective-permute-start(bf16[512,1024]{1,0:T(8,128)(2,1)} %get-tuple-element.29), channel_id=1, source_target_pairs={{0,1},{1,2},{2,3},{3,0},{4,5},{5,6},{6,7},{7,4},{8,9},{9,10},{10,1... | collective-permute-start | bytes 3145736 | tf_op jit(solution)/shard_map/ppermute | solution.py:220
  13.9 90.5 %collective-permute-start.1 = (bf16[512,1024]{1,0:T(8,128)(2,1)}, bf16[512,1024]{1,0:T(8,128)(2,1)}, u32[]{:S(2)}, u32[]{:S(2)}) collective-permute-start(bf16[512,1024]{1,0:T(8,128)(2,1)} %get-tuple-element.30), channel_id=1, source_target_pairs={{0,3},{1,0},{2,1},{3,2},{4,7},{5,4},{6,5},{7,6},{8,11},{9,8},{10,9... | collective-permute-start | bytes 3145736 | tf_op jit(solution)/shard_map/ppermute | solution.py:220
  16.8 103.2 %copy-start.5 = (f32[512,2,4]{0,2,1:T(4,128)}, f32[512,2,4]{0,2,1:T(4,128)S(1)}, u32[]{:S(2)}) copy-start(f32[512,2,4]{0,2,1:T(4,128)S(1)} %fusion.2) | copy-start | bytes 49156
  17.1 87.3 %copy-start.1 = (f32[512,2,4]{2,0,1:T(8,128)}, f32[512,2,4]{2,0,1:T(8,128)S(1)}, u32[]{:S(2)}) copy-start(f32[512,2,4]{2,0,1:T(8,128)S(1)} %copy.12) | copy-start | bytes 49156
  35.8 68.6 %copy-start.2 = (bf16[512,1024]{1,0:T(8,128)(2,1)}, bf16[512,1024]{1,0:T(8,128)(2,1)S(1)}, u32[]{:S(2)}) copy-start(bf16[512,1024]{1,0:T(8,128)(2,1)S(1)} %collective-permute-done.4.refs_5_) | copy-start | bytes 3145732
  35.8 68.6 %collective-permute-start.5 = (bf16[512,1024]{1,0:T(8,128)(2,1)S(1)}, bf16[512,1024]{1,0:T(8,128)(2,1)}, u32[]{:S(2)}, u32[]{:S(2)}) collective-permute-start(bf16[512,1024]{1,0:T(8,128)(2,1)S(1)} %collective-permute-done.4.refs_5_), channel_id=1, source_target_pairs={{0,3},{1,0},{2,1},{3,2},{4,7},{5,4},{6,5},{7,6},{8,11},{9,8},{10,9... | collective-permute-start | bytes 3145736 | tf_op jit(solution)/shard_map/ppermute | solution.py:221
  39.2 65.2 %copy-start.3 = (bf16[512,1024]{1,0:T(8,128)(2,1)}, bf16[512,1024]{1,0:T(8,128)(2,1)S(1)}, u32[]{:S(2)}) copy-start(bf16[512,1024]{1,0:T(8,128)(2,1)S(1)} %collective-permute-done.refs_1_) | copy-start | bytes 3145732
  39.2 65.2 %collective-permute-start.2 = (bf16[512,1024]{1,0:T(8,128)(2,1)S(1)}, bf16[512,1024]{1,0:T(8,128)(2,1)}, u32[]{:S(2)}, u32[]{:S(2)}) collective-permute-start(bf16[512,1024]{1,0:T(8,128)(2,1)S(1)} %collective-permute-done.refs_1_), channel_id=1, source_target_pairs={{0,1},{1,2},{2,3},{3,0},{4,5},{5,6},{6,7},{7,4},{8,9},{9,10},{10,1... | collective-permute-start | bytes 3145736 | tf_op jit(solution)/shard_map/ppermute | solution.py:221
  40.0 26.5 %all-to-all-start = ((f32[64,8,128]{2,1,0:T(8,128)}), f32[64,8,128]{2,1,0:T(8,128)S(1)}, u32[]{:S(2)}, u32[]{:S(2)}) async-start(f32[64,8,128]{2,1,0:T(8,128)} %broadcast_in_dim.30), calls=%async_computation | async-start | bytes 524288 | tf_op jit(solution)/shard_map/all_to_all | solution.py:228
  137.2 18.9 %all-to-all-start.2 = ((bf16[64,8,128]{2,1,0:T(8,128)(2,1)}), bf16[64,8,128]{2,1,0:T(8,128)(2,1)S(1)}, u32[]{:S(2)}, u32[]{:S(2)}) async-start(bf16[64,8,128]{2,1,0:T(8,128)(2,1)} %bitcast.11), calls=%async_computation.2 | async-start | bytes 262144 | tf_op jit(solution)/shard_map/all_to_all | solution.py:266
  156.1 0.7 copy-start.4
Sparse Core Ops, SparseCore 0:
  10.2 94.1 all-gather.1

commit v4 on v3

--- a/solution.py
+++ b/solution.py
@@ -97,21 +97,24 @@
             cols = slice(h * HEAD, (h + 1) * HEAD)
             for t in range(2):
                 rows = slice(t * half, (t + 1) * half)
-                wide = (t + 1) * half
-                scores = lax.dot_general(
-                    q[rows, cols],
-                    k[base : base + wide, cols],
-                    (((1,), (1,)), ((), ())),
-                    preferred_element_type=F32,
-                )
-                gap = run[b, rows, h : h + 1] - across[b, h : h + 1, :wide]
-                at = lax.broadcasted_iota(jnp.int32, gap.shape, 0) + t * half
-                lower = at >= lax.broadcasted_iota(jnp.int32, gap.shape, 1)
-                fading = jnp.exp(jnp.where(lower, gap, -1e30))
-                mix = (fading * scores).astype(BF16)
-                intra[base + t * half : base + wide, cols] = jnp.dot(
-                    mix, v[base : base + wide, cols], preferred_element_type=F32
-                )
+                total = None
+                for u in range(t + 1):
+                    seen = slice(base + u * half, base + (u + 1) * half)
+                    scores = lax.dot_general(
+                        q[rows, cols],
+                        k[seen, cols],
+                        (((1,), (1,)), ((), ())),
+                        preferred_element_type=F32,
+                    )
+                    gap = run[b, rows, h : h + 1] - across[b, h : h + 1, u * half : (u + 1) * half]
+                    if u == t:
+                        at = lax.broadcasted_iota(jnp.int32, gap.shape, 0)
+                        lower = at >= lax.broadcasted_iota(jnp.int32, gap.shape, 1)
+                        gap = jnp.where(lower, gap, -1e30)
+                    mix = (jnp.exp(gap) * scores).astype(BF16)
+                    part = jnp.dot(mix, v[seen, cols], preferred_element_type=F32)
+                    total = part if u == 0 else total + part
+                intra[base + t * half : base + (t + 1) * half, cols] = total
 
 
 def finish_kernel(q, intra, run, last, entry, fresh, out):

time: 169 us -> 169 us (level)
  transfers between devices with their start and end apart: 9 -> 9, of which waited for: 3 -> 3; matrix products, arithmetic and copies ran while one was open for 4% -> 4% of each run, Pallas kernels for 8% -> 9%
where the time goes in v4:
time: 169 us
  waiting for transfers between devices  66.5 us (39%)
  Pallas kernels  34.8 us (21%)
  starting transfers between devices  28.9 us (17%)
  blocking collectives  16.3 us (10%)
  between operations  13.6 us (8%)
  local copies, waits for them, and re-layouts  7.1 us (4%)
    all_gather x1, waiting for transfers between devices, on_device(): weights = lax.all_gather(projection, 'seq', axis=1, tiled=True)  36.2 us
    ppermute x2, waiting for transfers between devices, gather_tokens(): left0, right1 = (ahead(top), back(bottom))  18.7 us
    all_to_all x1, blocking collectives, prefixes(): piece = lax.all_to_all(state.reshape(n, -1, HEAD), 'seq', 0, 0, tiled=True)  16.3 us
    pallas_call x1, Pallas kernels, project_kv(): pl.pallas_call(kv_kernel, grid=(1,), in_specs=[SCALARS] + [LEFT] * 8 + [w...  15.5 us
    pallas_call x1, Pallas kernels, project_q(): pl.pallas_call(q_kernel, grid=(1,), in_specs=[SCALARS] + [LEFT] * 8 + [wh...  14.6 us
    all_to_all x1, starting transfers between devices, factors(): lax.all_to_all(jnp.broadcast_to(row, (n, 8, HEAD)), 'seq', 0, 0, tiled=True)  14.5 us
    all_to_all x1, waiting for transfers between devices, factors(): lax.all_to_all(jnp.broadcast_to(row, (n, 8, HEAD)), 'seq', 0, 0, tiled=True)  10.9 us
    all_to_all x1, starting transfers between devices, on_device(): entry = lax.all_to_all(prefix, 'seq', 0, 0, tiled=True).reshape(final.shape)  4.89 us
  transfers between devices with their start and end apart: 9, of which 3 were waited for; matrix products, arithmetic and copies ran while one was open for 4% of the time, Pallas kernels for 9%

profile of v4, /device:TPU:1, one launch (start us, length us, event | category | flops | bytes accessed | tf_op | source)
XLA Modules:
  0.0 168.9 jit_solution(10052247681190285207)
XLA Ops:
  6.5 0.0 copy-start
  6.5 0.0 all-gather.2.cloned.1.call-start
  6.5 0.7 all-gather.2.cloned.1.call-update
  7.3 0.0 copy-start.6
  7.3 3.1 %fusion.8 = (bf16[512,1024]{1,0:T(8,128)(2,1)}, bf16[512,1024]{1,0:T(8,128)(2,1)}) fusion(bf16[1024,1024]{1,0:T(8,128)(2,1)} %refs_0_.3), kind=kLoop, calls=%fused_computation.19 | loop fusion | bytes 4194304 | tf_op jit(solution)/shard_map/slice | solution.py:221
  10.4 3.3 %collective-permute-start.4 = (bf16[512,1024]{1,0:T(8,128)(2,1)}, bf16[512,1024]{1,0:T(8,128)(2,1)S(1)}, u32[]{:S(2)}, u32[]{:S(2)}) collective-permute-start(bf16[512,1024]{1,0:T(8,128)(2,1)} %get-tuple-element.29), channel_id=1, source_target_pairs={{0,3},{1,0},{2,1},{3,2},{4,7},{5,4},{6,5},{7,6},{8,11},{9,8},{10,9... | collective-permute-start | bytes 3145736 | tf_op jit(solution)/shard_map/ppermute | solution.py:222
  13.7 0.0 collective-permute-start
  13.7 0.2 collective-permute-start.3
  13.9 2.5 %collective-permute-start.1 = (bf16[512,1024]{1,0:T(8,128)(2,1)}, bf16[512,1024]{1,0:T(8,128)(2,1)}, u32[]{:S(2)}, u32[]{:S(2)}) collective-permute-start(bf16[512,1024]{1,0:T(8,128)(2,1)} %get-tuple-element.30), channel_id=1, source_target_pairs={{0,3},{1,0},{2,1},{3,2},{4,7},{5,4},{6,5},{7,6},{8,11},{9,8},{10,9... | collective-permute-start | bytes 3145736 | tf_op jit(solution)/shard_map/ppermute | solution.py:223
  16.4 0.0 copy-done
  16.4 0.4 fusion.2
  16.8 0.0 copy-start.5
  16.8 0.3 copy.12
  17.1 0.0 copy-start.1
  17.1 18.7 %collective-permute-done.4.refs_5_ = bf16[512,1024]{1,0:T(8,128)(2,1)S(1)} collective-permute-done((bf16[512,1024]{1,0:T(8,128)(2,1)}, bf16[512,1024]{1,0:T(8,128)(2,1)S(1)}, u32[]{:S(2)}, u32[]{:S(2)}) %collective-permute-start.4) | collective-permute-done | bytes 1048608 | tf_op jit(solution)/shard_map/ppermute | solution.py:222
  35.8 0.0 copy-start.2
  35.8 3.4 %collective-permute-start.5 = (bf16[512,1024]{1,0:T(8,128)(2,1)S(1)}, bf16[512,1024]{1,0:T(8,128)(2,1)}, u32[]{:S(2)}, u32[]{:S(2)}) collective-permute-start(bf16[512,1024]{1,0:T(8,128)(2,1)S(1)} %collective-permute-done.4.refs_5_), channel_id=1, source_target_pairs={{0,3},{1,0},{2,1},{3,2},{4,7},{5,4},{6,5},{7,6},{8,11},{9,8},{10,9... | collective-permute-start | bytes 3145736 | tf_op jit(solution)/shard_map/ppermute | solution.py:224
  39.2 0.0 collective-permute-done.refs_1_
  39.2 0.0 copy-start.3
  39.2 0.0 collective-permute-start.2
  39.3 0.8 broadcast_in_dim.30
  40.0 14.5 %all-to-all-start = ((f32[64,8,128]{2,1,0:T(8,128)}), f32[64,8,128]{2,1,0:T(8,128)S(1)}, u32[]{:S(2)}, u32[]{:S(2)}) async-start(f32[64,8,128]{2,1,0:T(8,128)} %broadcast_in_dim.30), calls=%async_computation | async-start | bytes 524288 | tf_op jit(solution)/shard_map/all_to_all | solution.py:231
  54.6 0.6 slice.28
  55.2 0.0 copy-done.6
  55.2 0.5 and_select_fusion.order
  55.7 10.9 %all-to-all-done = f32[64,8,128]{2,1,0:T(8,128)S(1)} async-done(((f32[64,8,128]{2,1,0:T(8,128)}), f32[64,8,128]{2,1,0:T(8,128)S(1)}, u32[]{:S(2)}, u32[]{:S(2)}) %all-to-all-start) | async-done | bytes 262176 | tf_op jit(solution)/shard_map/all_to_all | solution.py:231
  66.6 0.9 dynamic-slice_reduce_fusion
  67.6 0.6 select_reduce_fusion
  68.2 36.2 %all-gather.2.cloned.1.call-done.refs_7_ = bf16[3,4096,512]{2,1,0:T(8,128)(2,1)} async-done(((bf16[3,64,512]{2,1,0:T(8,128)(2,1)}), bf16[3,4096,512]{2,1,0:T(8,128)(2,1)}) %all-gather.2.cloned.1.call-update) | async-done | bytes 12582928 | tf_op jit(solution)/shard_map/all_gather | solution.py:252
  104.4 0.0 collective-permute-done.3.refs_4_
  104.4 0.0 collective-permute-done.1.refs_2_
  104.4 0.0 collective-permute-done.5.refs_6_
  104.4 0.0 collective-permute-done.2.refs_3_
  104.4 0.0 copy-done.1
  104.4 0.0 copy-done.2
  104.4 0.0 copy-done.3
  104.4 15.5 %keys_values.1 = (bf16[1024,512]{1,0:T(8,128)(2,1)}, bf16[1024,512]{1,0:T(8,128)(2,1)}, f32[4,128,128]{2,1,0:T(8,128)}, bf16[4,128,128]{2,1,0:T(8,128)(2,1)}) custom-call(s32[4]{0:T(128)} %and_select_fusion.order, bf16[1024,1024]{1,0:T(8,128)(2,1)} %refs_0_.3, bf16[512,1024]{1,0:T(8,128)(2,1)} %copy-done.3, ...), custom_call_target="tpu_custom_call" | custom-call | flops 8589934592 | bytes 20971520 | tf_op jit(solution)/shard_map/keys_values/pallas_call | solution.py:155
  119.9 0.0 copy-done.5
  120.0 16.3 %all_to_all.15 = bf16[64,8,128]{2,1,0:T(8,128)(2,1)S(1)} all-to-all(bf16[64,8,128]{2,1,0:T(8,128)(2,1)} %bitcast.28), channel_id=1, replica_groups=mesh['seq'=64,'fsdp'=4] {'seq'}, dimensions={0} | all-to-all | bytes 262144 | tf_op jit(solution)/shard_map/all_to_all | solution.py:242
  136.2 0.2 fusion
  136.5 0.7 copy.14
  137.2 4.9 %all-to-all-start.2 = ((bf16[64,8,128]{2,1,0:T(8,128)(2,1)}), bf16[64,8,128]{2,1,0:T(8,128)(2,1)S(1)}, u32[]{:S(2)}, u32[]{:S(2)}) async-start(bf16[64,8,128]{2,1,0:T(8,128)(2,1)} %bitcast.11), calls=%async_computation.2 | async-start | bytes 262144 | tf_op jit(solution)/shard_map/all_to_all | solution.py:269
  142.1 14.6 %queries.1 = (bf16[1024,512]{1,0:T(8,128)(2,1)}, f32[1024,512]{1,0:T(8,128)}) custom-call(s32[4]{0:T(128)} %and_select_fusion.order, bf16[1024,1024]{1,0:T(8,128)(2,1)} %refs_0_.3, bf16[512,1024]{1,0:T(8,128)(2,1)} %copy-done.3, bf16[512,1024]{1,0:T(8,128)(2,1)} %collective-permute-done.1.refs_2_, bf16[512,1024]{1,0:T(8,128)(2,1)} %collective-permute-done.2.refs_3_, ...), custom_call_target="tpu_custom_call" | custom-call | flops 4294967296 | bytes 20971520 | tf_op jit(solution)/shard_map/queries/pallas_call | solution.py:173
  156.7 0.0 all-to-all-done.2
  156.7 0.0 copy-start.4
  156.7 0.7 copy-done.4
  157.3 4.7 %finish.1 = bf16[1024,512]{1,0:T(8,128)(2,1)} custom-call(bf16[1024,512]{1,0:T(8,128)(2,1)} %get-tuple-element.24.q, f32[1024,512]{1,0:T(8,128)} %get-tuple-element.25.intra, f32[2,512,4]{2,1,0:T(8,128)} %bitcast.25, f32[2,4]{1,0:T(2,128)} %bitcast.31, bf16[4,128,128]{2,1,0:T(8,128)(2,1)} %bitcast.26, f32[4,128,128]{2,1,0:T(8,128)} %get-tuple-element.28.fresh), custom_call_target="tpu_custom_call" | custom-call | flops 268435456 | bytes 5242880 | tf_op jit(solution)/shard_map/finish/pallas_call | solution.py:193
  (5 shorter events, 0.1 us)
Async XLA Ops:
  6.5 9.8 %copy-start = (f32[1024,4]{0,1:T(4,128)S(1)}, f32[1024,4]{0,1:T(4,128)}, u32[]{:S(2)}) copy-start(f32[1024,4]{0,1:T(4,128)} %param.6) | copy-start | bytes 49156
  6.5 97.8 %all-gather.2.cloned.1.call-start = ((), (), s32[]{:S(2)}) async-start(), calls=%async_computation.3 | async-start | bytes 12779520 | tf_op jit(solution)/shard_map/all_gather | solution.py:252
  7.3 48.0 %copy-start.6 = (s32[4]{0:T(128)S(1)}, s32[4]{0:T(128)}, u32[]{:S(2)}) copy-start(s32[4]{0:T(128)} %constant.49.clone) | copy-start | bytes 52
  10.4 25.5 %collective-permute-start.4 = (bf16[512,1024]{1,0:T(8,128)(2,1)}, bf16[512,1024]{1,0:T(8,128)(2,1)S(1)}, u32[]{:S(2)}, u32[]{:S(2)}) collective-permute-start(bf16[512,1024]{1,0:T(8,128)(2,1)} %get-tuple-element.29), channel_id=1, source_target_pairs={{0,3},{1,0},{2,1},{3,2},{4,7},{5,4},{6,5},{7,6},{8,11},{9,8},{10,9... | collective-permute-start | bytes 3145736 | tf_op jit(solution)/shard_map/ppermute | solution.py:222
  13.7 25.6 %collective-permute-start = (bf16[512,1024]{1,0:T(8,128)(2,1)}, bf16[512,1024]{1,0:T(8,128)(2,1)S(1)}, u32[]{:S(2)}, u32[]{:S(2)}) collective-permute-start(bf16[512,1024]{1,0:T(8,128)(2,1)} %get-tuple-element.30), channel_id=1, source_target_pairs={{0,1},{1,2},{2,3},{3,0},{4,5},{5,6},{6,7},{7,4},{8,9},{9,10},{10,1... | collective-permute-start | bytes 3145736 | tf_op jit(solution)/shard_map/ppermute | solution.py:222
  13.7 90.7 %collective-permute-start.3 = (bf16[512,1024]{1,0:T(8,128)(2,1)}, bf16[512,1024]{1,0:T(8,128)(2,1)}, u32[]{:S(2)}, u32[]{:S(2)}) collective-permute-start(bf16[512,1024]{1,0:T(8,128)(2,1)} %get-tuple-element.29), channel_id=1, source_target_pairs={{0,1},{1,2},{2,3},{3,0},{4,5},{5,6},{6,7},{7,4},{8,9},{9,10},{10,1... | collective-permute-start | bytes 3145736 | tf_op jit(solution)/shard_map/ppermute | solution.py:223
  13.9 90.5 %collective-permute-start.1 = (bf16[512,1024]{1,0:T(8,128)(2,1)}, bf16[512,1024]{1,0:T(8,128)(2,1)}, u32[]{:S(2)}, u32[]{:S(2)}) collective-permute-start(bf16[512,1024]{1,0:T(8,128)(2,1)} %get-tuple-element.30), channel_id=1, source_target_pairs={{0,3},{1,0},{2,1},{3,2},{4,7},{5,4},{6,5},{7,6},{8,11},{9,8},{10,9... | collective-permute-start | bytes 3145736 | tf_op jit(solution)/shard_map/ppermute | solution.py:223
  16.8 103.2 %copy-start.5 = (f32[512,2,4]{0,2,1:T(4,128)}, f32[512,2,4]{0,2,1:T(4,128)S(1)}, u32[]{:S(2)}) copy-start(f32[512,2,4]{0,2,1:T(4,128)S(1)} %fusion.2) | copy-start | bytes 49156
  17.1 87.3 %copy-start.1 = (f32[512,2,4]{2,0,1:T(8,128)}, f32[512,2,4]{2,0,1:T(8,128)S(1)}, u32[]{:S(2)}) copy-start(f32[512,2,4]{2,0,1:T(8,128)S(1)} %copy.12) | copy-start | bytes 49156
  35.8 68.6 %copy-start.2 = (bf16[512,1024]{1,0:T(8,128)(2,1)}, bf16[512,1024]{1,0:T(8,128)(2,1)S(1)}, u32[]{:S(2)}) copy-start(bf16[512,1024]{1,0:T(8,128)(2,1)S(1)} %collective-permute-done.4.refs_5_) | copy-start | bytes 3145732
  35.8 68.6 %collective-permute-start.5 = (bf16[512,1024]{1,0:T(8,128)(2,1)S(1)}, bf16[512,1024]{1,0:T(8,128)(2,1)}, u32[]{:S(2)}, u32[]{:S(2)}) collective-permute-start(bf16[512,1024]{1,0:T(8,128)(2,1)S(1)} %collective-permute-done.4.refs_5_), channel_id=1, source_target_pairs={{0,3},{1,0},{2,1},{3,2},{4,7},{5,4},{6,5},{7,6},{8,11},{9,8},{10,9... | collective-permute-start | bytes 3145736 | tf_op jit(solution)/shard_map/ppermute | solution.py:224
  39.2 65.2 %copy-start.3 = (bf16[512,1024]{1,0:T(8,128)(2,1)}, bf16[512,1024]{1,0:T(8,128)(2,1)S(1)}, u32[]{:S(2)}) copy-start(bf16[512,1024]{1,0:T(8,128)(2,1)S(1)} %collective-permute-done.refs_1_) | copy-start | bytes 3145732
  39.2 65.2 %collective-permute-start.2 = (bf16[512,1024]{1,0:T(8,128)(2,1)S(1)}, bf16[512,1024]{1,0:T(8,128)(2,1)}, u32[]{:S(2)}, u32[]{:S(2)}) collective-permute-start(bf16[512,1024]{1,0:T(8,128)(2,1)S(1)} %collective-permute-done.refs_1_), channel_id=1, source_target_pairs={{0,1},{1,2},{2,3},{3,0},{4,5},{5,6},{6,7},{7,4},{8,9},{9,10},{10,1... | collective-permute-start | bytes 3145736 | tf_op jit(solution)/shard_map/ppermute | solution.py:224
  40.0 26.5 %all-to-all-start = ((f32[64,8,128]{2,1,0:T(8,128)}), f32[64,8,128]{2,1,0:T(8,128)S(1)}, u32[]{:S(2)}, u32[]{:S(2)}) async-start(f32[64,8,128]{2,1,0:T(8,128)} %broadcast_in_dim.30), calls=%async_computation | async-start | bytes 524288 | tf_op jit(solution)/shard_map/all_to_all | solution.py:231
  137.2 19.5 %all-to-all-start.2 = ((bf16[64,8,128]{2,1,0:T(8,128)(2,1)}), bf16[64,8,128]{2,1,0:T(8,128)(2,1)S(1)}, u32[]{:S(2)}, u32[]{:S(2)}) async-start(bf16[64,8,128]{2,1,0:T(8,128)(2,1)} %bitcast.11), calls=%async_computation.2 | async-start | bytes 262144 | tf_op jit(solution)/shard_map/all_to_all | solution.py:269
  156.7 0.7 copy-start.4
Sparse Core Ops, SparseCore 0:
  10.2 94.1 all-gather.1
